TPU v7x, 128 devices: a whole 4x4x4 slice. The times are simulated.
128 devices in a mesh: kb: 16 (over y, z), col: 8 (over x, core).
Axes of the slice: x: 4, y: 4, z: 4, core: 2. Of those that a mesh axis runs over, the one named last changes fastest.
Arguments:
- q_index: int32 [16384, 1], P(('kb', 'col')), may hold values from 0 to 127; in each aligned block of 128 rows (0 to 127, 128 to 255, ...) at most 2 rows name the same one
- cond_pairs: bfloat16 [16384, 16, 1200], P(('kb', 'col')), may hold values from -1 to 1
- val_pairs: bfloat16 [16384, 16, 1200], P(('kb', 'col')), may hold values from -1 to 1
- row_vc: bfloat16 [256, 16, 1200], P(('kb', 'col')), may hold values from -1 to 1
- col_vc: bfloat16 [64, 16, 1200], P('col'), may hold values from -1 to 1
- coulomb: float32 [1200], replicated, may hold values from 0.1 to 3
- screened: bfloat16 [128, 1200, 1200], P(('kb', 'col')), may hold values from -0.1875 to 0.1875
Outputs:
- kernel: float32 [16384, 256], P(('kb', 'col'))
Inputs may be any that keep to these rules, and one draw needn't show every extreme that they name: `q_index`: among the 128 pairs of one device (aligned blocks of rows) no momentum transfer occurs more than 2 times, a bound that some block reaches; every momentum transfer occurs somewhere.
All inputs are finite; a program needn't handle non-finite values.
Results may differ from a plain program's by a relative error of at most 0.0029.
Values may be sent and summed in bfloat16 or wider, within the bound.
A program may use at most 192 MiB of HBM per device.

v0:
```python
import jax
import jax.numpy as jnp
from jax import lax
from jax.sharding import PartitionSpec as P

NV = 4
NC = 4


def shards(q_index, cond_pairs, val_pairs, row_vc, col_vc, coulomb, screened):
    n_rows = lax.axis_size("kb")
    n_cols = lax.axis_size("col")
    devices = n_rows * n_cols
    count = cond_pairs.shape[0]
    width = cond_pairs.shape[2]
    slots = max(2, (2 * count + devices - 1) // devices)
    target = q_index[:, 0]
    onehot = (target[:, None] == jnp.arange(devices, dtype=jnp.int32)[None, :]).astype(jnp.int32)
    before = jnp.cumsum(onehot, axis=0) - onehot
    rank = jnp.sum(before * onehot, axis=1)
    place = target * slots + rank
    send_cond = jnp.zeros((devices * slots, NC * NC, width), jnp.bfloat16).at[place].set(cond_pairs)
    send_val = jnp.zeros((devices * slots, NV * NV, width), jnp.bfloat16).at[place].set(val_pairs)
    wlocal = screened[0]
    recv_cond = lax.all_to_all(
        send_cond.reshape(devices, slots, NC * NC, width),
        ("kb", "col"),
        split_axis=0,
        concat_axis=0,
        tiled=True,
    )
    recv_val = lax.all_to_all(
        send_val.reshape(devices, slots, NV * NV, width),
        ("kb", "col"),
        split_axis=0,
        concat_axis=0,
        tiled=True,
    )
    applied = jnp.einsum(
        "dsvh,gh->dsvg", recv_val, wlocal, preferred_element_type=jnp.float32
    ).astype(jnp.bfloat16)
    terms = jnp.einsum("dscg,dsvg->dscv", recv_cond, applied, preferred_element_type=jnp.float32)
    results = terms.reshape(terms.shape[0], terms.shape[1], NC * NC * NV * NV)
    returned = lax.all_to_all(results, ("kb", "col"), split_axis=0, concat_axis=0, tiled=True)
    direct = returned.reshape(devices * slots, NC * NC * NV * NV)[place]
    direct = (
        direct.reshape(count, NC, NC, NV, NV)
        .transpose(0, 3, 1, 4, 2)
        .reshape(count, NV * NC * NV * NC)
    )
    scaled = (col_vc.astype(jnp.float32) * coulomb[None, None, :]).astype(jnp.bfloat16)
    exchange = jnp.einsum(
        "avg,bwg->abvw",
        lax.all_gather(row_vc, "col", axis=0, tiled=True),
        scaled,
        preferred_element_type=jnp.float32,
    )
    exchange = exchange.reshape(count, NV * NC * NV * NC)
    return 2.0 * exchange - direct


def solution(mesh):
    return jax.shard_map(
        shards,
        mesh=mesh,
        in_specs=(
            P(("kb", "col"), None),
            P(("kb", "col"), None, None),
            P(("kb", "col"), None, None),
            P(("kb", "col"), None, None),
            P("col", None, None),
            P(),
            P(("kb", "col"), None, None),
        ),
        out_specs=P(("kb", "col"), None),
        check_vma=False,
    )
```

profile of v0, /device:TPU:0, one launch (start us, length us, event | category | flops | bytes accessed | tf_op | source)
XLA Modules:
  0.0 405.7 jit_solution(5232399124069101491)
XLA Ops:
  0.0 0.9 fusion.7
  2.6 8.7 %copy.38 = bf16[128,16,1200]{2,1,0:T(8,128)(2,1)} copy(bf16[128,16,1200]{0,2,1:T(8,128)(2,1)} %param.9) | data formatting | bytes 9830400 | tf_op args[2]
  11.2 4.5 %broadcast.20.clone.1 = bf16[256,16,1200]{2,1,0:T(8,128)(2,1)} broadcast(bf16[]{:T(256)} %constant.6.clone.1), dimensions={} | broadcast | bytes 9830402 | tf_op jit(solution)/shard_map/broadcast.5
  15.7 20.4 %scatter_fusion.1 = bf16[256,16,1200]{2,1,0:T(8,128)(2,1)} fusion(bf16[256,16,1200]{2,1,0:T(8,128)(2,1)} %broadcast.20.clone.1, s32[128]{0:T(128)S(1)} %fusion.8, bf16[128,16,1200]{2,1,0:T(8,128)(2,1)} %copy.38), kind=kCustom, calls=%fused_computation.2 | custom fusion | bytes 14746112 | tf_op jit(solution)/shard_map/scatter | solution.py:23
  36.2 11.7 %all-to-all-start.1 = ((bf16[128,2,16,1200]{3,2,1,0:T(8,128)(2,1)}), bf16[128,2,16,1200]{3,2,1,0:T(8,128)(2,1)}, u32[]{:S(2)}, u32[]{:S(2)}) async-start(bf16[128,2,16,1200]{3,2,1,0:T(8,128)(2,1)} %bitcast.36), calls=%async_computation.1 | async-start | bytes 20971520 | tf_op jit(solution)/shard_map/all_to_all | solution.py:32
  47.8 8.7 %copy.37 = bf16[128,16,1200]{2,1,0:T(8,128)(2,1)} copy(bf16[128,16,1200]{0,2,1:T(8,128)(2,1)} %param.8) | data formatting | bytes 9830400 | tf_op args[1]
  56.6 4.6 %broadcast.20.clone = bf16[256,16,1200]{2,1,0:T(8,128)(2,1)} broadcast(bf16[]{:T(256)} %constant.6.clone.1), dimensions={} | broadcast | bytes 9830402 | tf_op jit(solution)/shard_map/broadcast.5
  61.2 20.6 %scatter_fusion = bf16[256,16,1200]{2,1,0:T(8,128)(2,1)} fusion(bf16[256,16,1200]{2,1,0:T(8,128)(2,1)} %broadcast.20.clone, s32[128]{0:T(128)S(1)} %fusion.8, bf16[128,16,1200]{2,1,0:T(8,128)(2,1)} %copy.37), kind=kCustom, calls=%fused_computation.1 | custom fusion | bytes 14746112 | tf_op jit(solution)/shard_map/scatter | solution.py:22
  81.8 92.8 %all-to-all-done.1 = bf16[128,2,16,1200]{3,2,1,0:T(8,128)(2,1)} async-done(((bf16[128,2,16,1200]{3,2,1,0:T(8,128)(2,1)}), bf16[128,2,16,1200]{3,2,1,0:T(8,128)(2,1)}, u32[]{:S(2)}, u32[]{:S(2)}) %all-to-all-start.1) | async-done | bytes 9830432 | tf_op jit(solution)/shard_map/all_to_all | solution.py:32
  174.6 17.1 %all-to-all-start = ((bf16[128,2,16,1200]{3,2,1,0:T(8,128)(2,1)}), bf16[128,2,16,1200]{3,2,1,0:T(8,128)(2,1)}, u32[]{:S(2)}, u32[]{:S(2)}) async-start(bf16[128,2,16,1200]{3,2,1,0:T(8,128)(2,1)} %bitcast.35), calls=%async_computation | async-start | bytes 20971520 | tf_op jit(solution)/shard_map/all_to_all | solution.py:25
  191.7 132.7 %all_gather.3 = bf16[16,16,1200]{2,1,0:T(8,128)(2,1)} all-gather(bf16[2,16,1200]{2,1,0:T(8,128)(2,1)S(1)} %copy-done.2), channel_id=1, replica_groups=mesh['kb'=16,'col'=8] {'col'}, dimensions={0}, use_global_device_ids=true | all-gather | bytes 691200 | tf_op jit(solution)/shard_map/all_gather | solution.py:54
  324.5 17.2 %convolution_convert_fusion = bf16[128,2,16,1200]{0,3,2,1:T(8,128)(2,1)} fusion(bf16[128,2,16,1200]{3,2,1,0:T(8,128)(2,1)} %all-to-all-done.1, bf16[1,1200,1200]{2,1,0:T(8,128)(2,1)S(1)} %copy-done), kind=kOutput, calls=%fused_computation.3 | convolution fusion | flops 11801395200 | bytes 22540800 | tf_op jit(solution)/shard_map/dsvh,gh->dsvg/dot_general | solution.py:39
  341.7 16.5 %copy.40 = bf16[128,2,16,1200]{3,2,1,0:T(8,128)(2,1)} copy(bf16[128,2,16,1200]{0,3,2,1:T(8,128)(2,1)} %convolution_convert_fusion) | data formatting | bytes 19660800 | tf_op jit(solution)/shard_map/convert_element_type | solution.py:41
  358.1 11.1 %fusion.9 = f32[128,2,16,16]{3,2,1,0:T(8,128)} fusion(bf16[128,2,16,1200]{3,2,1,0:T(8,128)(2,1)} %all-to-all-done, bf16[128,2,16,1200]{3,2,1,0:T(8,128)(2,1)} %copy.40), kind=kOutput, calls=%fused_computation.19 | convolution fusion | flops 157286400 | bytes 19922944 | tf_op jit(solution)/shard_map/dscg,dsvg->dscv/dot_general | solution.py:42
  369.2 2.7 copy.41
  371.9 0.8 copy.42
  372.7 18.4 %all-to-all-start.2 = ((f32[128,2,256]{2,1,0:T(2,128)}), f32[128,2,256]{2,1,0:T(2,128)}, u32[]{:S(2)}, u32[]{:S(2)}) async-start(f32[128,2,256]{2,1,0:T(2,128)} %copy.42), calls=%async_computation.2 | async-start | bytes 524288 | tf_op jit(solution)/shard_map/all_to_all | solution.py:44
  391.1 3.1 fusion.2
  394.2 2.6 copy.36
  396.8 1.6 mul.35
  398.4 3.0 all-to-all-done.2
  401.4 1.1 reshape.26
  402.5 1.4 gather_fusion
  403.9 1.0 copy.43
  (16 shorter events, 2.5 us)
Async XLA Ops:
  0.0 324.5 %copy-start = (bf16[1,1200,1200]{2,1,0:T(8,128)(2,1)S(1)}, bf16[1,1200,1200]{2,1,0:T(8,128)(2,1)}, u32[]{:S(2)}) copy-start(bf16[1,1200,1200]{2,1,0:T(8,128)(2,1)} %param.13) | copy-start | bytes 8640004
  36.2 138.4 %all-to-all-start.1 = ((bf16[128,2,16,1200]{3,2,1,0:T(8,128)(2,1)}), bf16[128,2,16,1200]{3,2,1,0:T(8,128)(2,1)}, u32[]{:S(2)}, u32[]{:S(2)}) async-start(bf16[128,2,16,1200]{3,2,1,0:T(8,128)(2,1)} %bitcast.36), calls=%async_computation.1 | async-start | bytes 20971520 | tf_op jit(solution)/shard_map/all_to_all | solution.py:32
  174.6 17.1 %copy-start.2 = (bf16[2,16,1200]{2,1,0:T(8,128)(2,1)S(1)}, bf16[2,16,1200]{2,1,0:T(8,128)(2,1)}, u32[]{:S(2)}) copy-start(bf16[2,16,1200]{2,1,0:T(8,128)(2,1)} %param.10) | copy-start | bytes 230404
  174.6 183.5 %all-to-all-start = ((bf16[128,2,16,1200]{3,2,1,0:T(8,128)(2,1)}), bf16[128,2,16,1200]{3,2,1,0:T(8,128)(2,1)}, u32[]{:S(2)}, u32[]{:S(2)}) async-start(bf16[128,2,16,1200]{3,2,1,0:T(8,128)(2,1)} %bitcast.35), calls=%async_computation | async-start | bytes 20971520 | tf_op jit(solution)/shard_map/all_to_all | solution.py:25
  358.1 32.9 %copy-start.3 = (f32[1200]{0:T(1024)S(1)}, f32[1200]{0:T(1024)}, u32[]{:S(2)}) copy-start(f32[1200]{0:T(1024)} %param.12) | copy-start | bytes 14404
  358.1 47.6 %copy-start.1 = (bf16[1,1200,1200]{2,1,0:T(8,128)(2,1)S(1)}, bf16[1,1200,1200]{2,1,0:T(8,128)(2,1)}, u32[]{:S(2)}) copy-start(bf16[1,1200,1200]{2,1,0:T(8,128)(2,1)} %param.13) | copy-start | bytes 8640004
  372.7 28.7 %all-to-all-start.2 = ((f32[128,2,256]{2,1,0:T(2,128)}), f32[128,2,256]{2,1,0:T(2,128)}, u32[]{:S(2)}, u32[]{:S(2)}) async-start(f32[128,2,256]{2,1,0:T(2,128)} %copy.42), calls=%async_computation.2 | async-start | bytes 524288 | tf_op jit(solution)/shard_map/all_to_all | solution.py:44
where the time goes:
time: 408 us; the launch traced here: 406 us
  blocking collectives  133 us (33%)
  waiting for transfers between devices  95.7 us (23%)
  local copies, waits for them, and re-layouts  95.4 us (23%)
  starting transfers between devices  47.1 us (12%)
  matrix products  31.4 us (8%)
    all_gather x1, blocking collectives, shards(): lax.all_gather(row_vc, 'col', axis=0, tiled=True)  133 us
    all_to_all x1, waiting for transfers between devices, shards(): lax.all_to_all(send_val.reshape(devices, slots, NV * NV, width), ('kb', '...  92.8 us
    scatter x1, local copies, waits for them, and re-layouts, shards(): jnp.zeros((devices * slots, NC * NC, width), jnp.bfloat16).at[place]  20.6 us
    scatter x1, local copies, waits for them, and re-layouts, shards(): jnp.zeros((devices * slots, NV * NV, width), jnp.bfloat16).at[place]  20.4 us
    all_to_all x1, starting transfers between devices, shards(): lax.all_to_all(results, ('kb', 'col'), split_axis=0, concat_axis=0, tiled...  18.4 us
    unnamed x10, local copies, waits for them, and re-layouts  17.4 us
    dot_general x1, matrix products, shards(): jnp.einsum('dsvh,gh->dsvg', recv_val, wlocal, preferred_element_type=jnp....  17.2 us
    all_to_all x1, starting transfers between devices, shards(): lax.all_to_all(send_cond.reshape(devices, slots, NC * NC, width), ('kb',...  17.1 us
  transfers between devices with their start and end apart: 3, of which 2 were waited for; matrix products, arithmetic and copies ran while one was open for 18% of the time, Pallas kernels for 0%

commit v1 on v0

v1 whole, which is shorter than its diff:
```python
import functools

import jax
import jax.numpy as jnp
from jax import lax
from jax.experimental import pallas as pl
from jax.experimental.pallas import tpu as pltpu
from jax.sharding import PartitionSpec as P

MESH = pl.DeviceIdType.MESH
Z, Y, X = 0, 1, 2
ORDERS = ((X, Y, Z), (Y, Z, X), (Z, X, Y))
SLOTS = 4
MAIN = 1152
WIDE = 1280


def streams(cols):
    third = 384
    cuts = (0, third, 2 * third, cols)
    out = [(j, ORDERS[j], 0, cols) for j in range(3)]
    return out + [(3, ORDERS[i], cuts[i], cuts[i + 1]) for i in range(3)]


def at_axis(ref, lead, axis, index, c0, c1):
    where = [slice(None)] * 3
    where[axis] = index
    return ref.at[(lead, *where, slice(None), slice(c0, c1))]


def place_kernel(
    tab, val_hbm, cond_hbm, tail_ref, w_hbm,
    out_ref, r1v, r2v, r1c, r2c,
    vin, sv, sc, fv, fc, w2, tt, zbuf, dbuf,
    in_sem, w_sem, send, recv, last, local, back_send, back_recv,
):
    kb = lax.axis_index("kb")
    col = lax.axis_index("col")
    here = (kb & 3, kb >> 2, col >> 1)
    core = col & 1
    n_dev = 128

    def dev(chip, which):
        return (chip[Y] * 4 + chip[Z], chip[X] * 2 + which)

    def moved(axis, index):
        chip = list(here)
        chip[axis] = index
        return tuple(chip)

    barrier = pltpu.get_barrier_semaphore()
    me = kb * 8 + col

    load_val = pltpu.make_async_copy(val_hbm, vin, in_sem.at[0])
    load_val.start()
    load_w = pltpu.make_async_copy(w_hbm, w2.at[core], in_sem.at[1])
    load_w.start()

    @pl.loop(1, n_dev)
    def _(k):
        t = me ^ k
        pl.semaphore_signal(barrier, inc=1, device_id=(t >> 3, t & 7), device_id_type=MESH)

    load_val.wait()

    @pl.loop(0, 64)
    def _(chip):
        z, y, x = chip >> 4, (chip >> 2) & 3, chip & 3
        for j in range(SLOTS):
            p = tab[j * 64 + chip]
            sv[j, z, y, x, :, :MAIN] = vin[p, :, :MAIN]
            sv[j, z, y, x, :, MAIN:] = tail_ref[p]

    pl.semaphore_wait(barrier, n_dev - 1)
    load_cond = pltpu.make_async_copy(cond_hbm, vin, in_sem.at[0])
    load_cond.start()
    send_w = pltpu.make_async_remote_copy(
        w_hbm, w2.at[core], w_sem.at[0], w_sem.at[1], device_id=dev(here, 1 - core), device_id_type=MESH
    )
    send_w.start()

    rounds = ((sv, r1v, r2v, fv), (sc, r1c, r2c, fc))
    parts = (streams(WIDE), streams(MAIN))

    def ring(r, s, k, d):
        j, order, c0, c1 = parts[r][s]
        axis = order[k]
        src, dst = rounds[r][k], rounds[r][k + 1]
        there = (here[axis] + d) & 3
        return pltpu.make_async_remote_copy(
            at_axis(src, j, axis, there, c0, c1),
            at_axis(dst, j, axis, here[axis], c0, c1),
            send.at[r, s, k, d], recv.at[r, s, k, d],
            device_id=dev(moved(axis, there), core), device_id_type=MESH,
        )

    def keep(r, s, k):
        j, order, c0, c1 = parts[r][s]
        axis = order[k]
        return pltpu.make_async_copy(
            at_axis(rounds[r][k], j, axis, here[axis], c0, c1),
            at_axis(rounds[r][k + 1], j, axis, here[axis], c0, c1),
            local.at[r, s, k],
        )

    def start_ring(r, k):
        for s in range(6):
            keep(r, s, k).start()
        for d in (1, 3, 2):
            for s in range(6):
                ring(r, s, k, d).start()

    def wait_ring(r, k):
        for s in range(6):
            for d in (1, 3, 2):
                c = ring(r, s, k, d)
                c.wait_send()
                c.wait_recv()
            keep(r, s, k).wait()

    def final(r, s, d):
        j, order, c0, c1 = parts[r][s]
        axis = order[2]
        there = (here[axis] + d) & 3
        lead, goal = (core, j) if j < 2 else (j, core)
        src = at_axis(rounds[r][2], j, axis, there, c0, c1)
        dst = at_axis(rounds[r][3], lead, axis, here[axis], c0, c1)
        sem = last.at[r, lead, d] if j < 2 else last.at[r, s, d]
        return pltpu.make_async_remote_copy(
            src, dst, send.at[r, s, 2, d], sem,
            device_id=dev(moved(axis, there), goal), device_id_type=MESH,
        )

    def final_local(r, s):
        j, order, c0, c1 = parts[r][s]
        axis = order[2]
        lead = core if j < 2 else j
        return pltpu.make_async_copy(
            at_axis(rounds[r][2], j, axis, here[axis], c0, c1),
            at_axis(rounds[r][3], lead, axis, here[axis], c0, c1),
            local.at[r, s, 2],
        )

    def start_final(r):
        for s in range(6):
            if s < 2:
                @pl.when(core == s)
                def _():
                    final_local(r, s).start()

                @pl.when(core != s)
                def _():
                    final(r, s, 0).start()
            else:
                final_local(r, s).start()
        for d in (1, 3, 2):
            for s in range(6):
                final(r, s, d).start()

    def wait_final(r):
        for s in range(6):
            for d in (1, 3, 2):
                final(r, s, d).wait_send()
            if s < 2:
                @pl.when(core == s)
                def _():
                    final_local(r, s).wait()

                @pl.when(core != s)
                def _():
                    final(r, s, 0).wait_send()
            else:
                final_local(r, s).wait()
                for d in (1, 3, 2):
                    final(r, s, d).wait_recv()
        for mine in range(2):
            axis = ORDERS[mine][2]

            @pl.when(core == mine)
            def _():
                for lead in range(2):
                    for d in (1, 3, 2) if lead == mine else (1, 3, 2, 0):
                        at = at_axis(rounds[r][3], lead, axis, here[axis], 0, parts[r][0][3])
                        pltpu.make_async_remote_copy(
                            at, at, send.at[r, mine, 2, d], last.at[r, lead, d],
                            device_id=dev(here, 1 - core), device_id_type=MESH,
                        ).wait_recv()

    start_ring(0, 0)
    load_cond.wait()

    @pl.loop(0, 64)
    def _(chip):
        z, y, x = chip >> 4, (chip >> 2) & 3, chip & 3
        for j in range(SLOTS):
            p = tab[j * 64 + chip]
            sc[j, z, y, x] = vin[p, :, :MAIN]

    start_ring(1, 0)
    wait_ring(0, 0)
    start_ring(0, 1)
    wait_ring(1, 0)
    start_ring(1, 1)
    wait_ring(0, 1)
    start_final(0)
    load_w.wait()
    send_w.wait()
    wait_ring(1, 1)
    start_final(1)
    wait_final(0)

    group = lax.broadcasted_iota(jnp.int32, (16, 256), 1) >> 4
    row = lax.broadcasted_iota(jnp.int32, (16, 256), 0)
    nt = (((1,), (1,)), ((), ()))

    def diagonal(full):
        total = jnp.zeros((16, 256), jnp.float32)
        for i in range(16):
            total = jnp.where(group == i, full[16 * i : 16 * i + 16], total)
        return total

    @pl.loop(0, 16)
    def _(i):
        b, z = i >> 2, i & 3
        which = jnp.where(b < 2, core, b - 2)
        x = fv[b, z].reshape(256, WIDE)
        for n in range(5):
            w = w2[which, n * 256 : n * 256 + 256, :]
            part = lax.dot_general(x, w, nt, preferred_element_type=jnp.float32).astype(jnp.bfloat16)
            sv[b, z, :, :, :, n * 256 : n * 256 + 256] = part.reshape(4, 4, 16, 256)
            if n == 4:
                full = lax.dot_general(x[:, MAIN:], part[:, 128:], nt, preferred_element_type=jnp.float32)
                tt[b, z] = diagonal(full)

    wait_final(1)

    @pl.loop(0, 16)
    def _(i):
        b, z = i >> 2, i & 3
        full = lax.dot_general(
            fc[b, z].reshape(256, MAIN),
            sv[b, z, :, :, :, :MAIN].reshape(256, MAIN),
            nt,
            preferred_element_type=jnp.float32,
        )
        got = diagonal(full) + tt[b, z]
        turned = jnp.where(group == row, got, 0.0)
        for k in range(1, 16):
            shifted = pltpu.roll(pltpu.roll(got, 16 - k, 0), 16 * k, 1)
            turned = jnp.where(group == ((row + k) & 15), shifted, turned)
        for slot in range(16):
            zbuf[b, z, slot >> 2, slot & 3, 0:1] = turned[slot : slot + 1, :128]
            zbuf[b, z, slot >> 2, slot & 3, 1:2] = turned[slot : slot + 1, 128:]
        back_core = jnp.where(b < 2, b, core)
        back_slot = jnp.where(b < 2, core, b)

        @pl.loop(0, 16)
        def _(slot):
            y, x = slot >> 2, slot & 3
            mine = (z == here[Z]) & (y == here[Y]) & (x == here[X]) & (back_core == core)
            src = zbuf.at[b, z, y, x]
            dst = dbuf.at[back_slot, here[Z], here[Y], here[X]]

            @pl.when(mine)
            def _():
                pltpu.make_async_copy(src, dst, back_recv).start()

            @pl.when(jnp.logical_not(mine))
            def _():
                pltpu.make_async_remote_copy(
                    src, dst, back_send, back_recv,
                    device_id=dev((z, y, x), back_core), device_id_type=MESH,
                ).start()

    spot = zbuf.at[0, 0, 0, 0]

    @pl.loop(0, 64 * SLOTS - (SLOTS - 1))
    def _(_):
        pltpu.make_async_copy(spot, spot, back_send).wait()

    pltpu.make_async_copy(dbuf, dbuf, back_recv).wait()
    out_ref[...] = dbuf[...]


def direct_terms(tab, val_pairs, cond_pairs, tails, w_pad):
    any_spec = pl.BlockSpec(memory_space=pl.ANY)
    wide = (SLOTS, 4, 4, 4, 16, WIDE)
    main = (SLOTS, 4, 4, 4, 16, MAIN)
    bf16 = jnp.bfloat16
    small = (SLOTS, 4, 4, 4, 2, 128)
    out = pl.pallas_call(
        place_kernel,
        out_shape=(
            jax.ShapeDtypeStruct(small, jnp.float32),
            jax.ShapeDtypeStruct(wide, bf16),
            jax.ShapeDtypeStruct(wide, bf16),
            jax.ShapeDtypeStruct(main, bf16),
            jax.ShapeDtypeStruct(main, bf16),
        ),
        in_specs=[
            pl.BlockSpec(memory_space=pltpu.SMEM),
            any_spec,
            any_spec,
            pl.BlockSpec(memory_space=pltpu.VMEM),
            any_spec,
        ],
        out_specs=(pl.BlockSpec(memory_space=pltpu.VMEM), any_spec, any_spec, any_spec, any_spec),
        scratch_shapes=[
            pltpu.VMEM(val_pairs.shape, bf16),
            pltpu.VMEM(wide, bf16),
            pltpu.VMEM(main, bf16),
            pltpu.VMEM(wide, bf16),
            pltpu.VMEM(main, bf16),
            pltpu.VMEM((2, WIDE, WIDE), bf16),
            pltpu.VMEM((SLOTS, 4, 16, 256), jnp.float32),
            pltpu.VMEM(small, jnp.float32),
            pltpu.VMEM(small, jnp.float32),
            pltpu.SemaphoreType.DMA((2,)),
            pltpu.SemaphoreType.DMA((2,)),
            pltpu.SemaphoreType.DMA((2, 6, 3, 4)),
            pltpu.SemaphoreType.DMA((2, 6, 2, 4)),
            pltpu.SemaphoreType.DMA((2, 6, 4)),
            pltpu.SemaphoreType.DMA((2, 6, 3)),
            pltpu.SemaphoreType.DMA,
            pltpu.SemaphoreType.DMA,
        ],
        compiler_params=pltpu.CompilerParams(
            collective_id=0, has_side_effects=True, vmem_limit_bytes=60 * 2**20
        ),
    )(tab, val_pairs, cond_pairs, tails, w_pad)
    return out[0].reshape(SLOTS * 64, 256)


def shards(q_index, cond_pairs, val_pairs, row_vc, col_vc, coulomb, screened):
    count = cond_pairs.shape[0]
    target = q_index[:, 0]
    same = target[:, None] == target[None, :]
    earlier = jnp.arange(count)[None, :] < jnp.arange(count)[:, None]
    rank = jnp.sum((same & earlier).astype(jnp.int32), axis=1)
    core, x, z, y = target & 1, (target >> 1) & 3, (target >> 3) & 3, (target >> 5) & 3
    place = (rank * 2 + core) * 64 + (z * 4 + y) * 4 + x
    spots = jnp.arange(SLOTS * 64, dtype=jnp.int32)
    tab = jnp.sum(
        jnp.where(place[None, :] == spots[:, None], jnp.arange(count, dtype=jnp.int32)[None, :], 0), axis=1
    )
    gap = jnp.zeros((count, 16, 16), jnp.bfloat16)
    tails = jnp.concatenate([val_pairs[:, :, MAIN:], gap, cond_pairs[:, :, MAIN:], gap], axis=2)
    w = jnp.pad(screened[0], ((0, 0), (0, WIDE - screened.shape[2])))
    w_pad = jnp.concatenate(
        [w[:MAIN], jnp.zeros((64, WIDE), jnp.bfloat16), w[MAIN:], jnp.zeros((16, WIDE), jnp.bfloat16)], axis=0
    )
    direct = direct_terms(tab, val_pairs, cond_pairs, tails, w_pad)[place]
    direct = direct.reshape(count, 4, 4, 4, 4).transpose(0, 3, 1, 4, 2).reshape(count, 256)
    scaled = (col_vc.astype(jnp.float32) * coulomb[None, None, :]).astype(jnp.bfloat16)
    exchange = jnp.einsum(
        "avg,bwg->abvw",
        lax.all_gather(row_vc, "col", axis=0, tiled=True),
        scaled,
        preferred_element_type=jnp.float32,
    )
    return 2.0 * exchange.reshape(count, 256) - direct


def solution(mesh):
    return jax.shard_map(
        shards,
        mesh=mesh,
        in_specs=(
            P(("kb", "col"), None),
            P(("kb", "col"), None, None),
            P(("kb", "col"), None, None),
            P(("kb", "col"), None, None),
            P("col", None, None),
            P(),
            P(("kb", "col"), None, None),
        ),
        out_specs=P(("kb", "col"), None),
        check_vma=False,
    )
```

time: 408 us -> 307 us (0.75)
  Pallas kernels: 0 us -> 263 us
  blocking collectives: 133 us -> 13.2 us
  waiting for transfers between devices: 95.7 us -> 0 us
  local copies, waits for them, and re-layouts: 95.4 us -> 21.8 us
  starting transfers between devices: 47.1 us -> 0 us
  matrix products: 31.4 us -> 0.93 us
    pallas_call x0 -> x1, Pallas kernels: none -> 263 us  [direct_terms(): pl.pallas_call(place_kernel, out_shape=(jax.ShapeDtypeStruct(small, jnp.f...]
    all_gather x1, blocking collectives: 133 us -> 13.2 us  [shards(): lax.all_gather(row_vc, 'col', axis=0, tiled=True)]
    all_to_all x3 -> x0, waiting for transfers between devices: 95.7 us -> none  [the longest x1 92.8 us: shards(): lax.all_to_all(send_val.reshape(devices, slots, NV * NV, width), ('kb', '...]
    all_to_all x3 -> x0, starting transfers between devices: 47.1 us -> none  [the longest x1 18.4 us: shards(): lax.all_to_all(results, ('kb', 'col'), split_axis=0, concat_axis=0, tiled...]
    scatter x2 -> x0, local copies, waits for them, and re-layouts: 41.1 us -> none  [the longest x1 20.6 us: shards(): jnp.zeros((devices * slots, NC * NC, width), jnp.bfloat16).at[place]]
    dot_general x2 -> x0, matrix products: 28.3 us -> none  [the longest x1 17.2 us: shards(): jnp.einsum('dsvh,gh->dsvg', recv_val, wlocal, preferred_element_type=jnp....]
    convert_element_type x1 -> x0, local copies, waits for them, and re-layouts: 16.5 us -> none  [shards(): applied = jnp.einsum('dsvh,gh->dsvg', recv_val, wlocal, preferred_element...]
    another operation x2 -> x0, local copies, waits for them, and re-layouts: 9.15 us -> none
  transfers between devices with their start and end apart: 3 -> 0, of which waited for: 2 -> 0; matrix products, arithmetic and copies ran while one was open for 18% -> 0% of each run, Pallas kernels for 0% -> 0%
where the time goes in v1:
time: 307 us; the launch traced here: 305 us
  Pallas kernels  263 us (86%)
  local copies, waits for them, and re-layouts  21.8 us (7%)
  blocking collectives  13.2 us (4%)
  other arithmetic  5.99 us (2%)
    pallas_call x1, Pallas kernels, direct_terms(): pl.pallas_call(place_kernel, out_shape=(jax.ShapeDtypeStruct(small, jnp.f...  263 us
    unnamed x13, local copies, waits for them, and re-layouts  18.4 us
    all_gather x1, blocking collectives, shards(): lax.all_gather(row_vc, 'col', axis=0, tiled=True)  13.2 us

profile of v1, /device:TPU:0, one launch (start us, length us, event | category | flops | bytes accessed | tf_op | source)
XLA Modules:
  0.0 304.8 jit_solution(1989556892963066810)
XLA Ops:
  0.0 8.7 %copy.32.val_hbm = bf16[128,16,1200]{2,1,0:T(8,128)(2,1)} copy(bf16[128,16,1200]{0,2,1:T(8,128)(2,1)} %param.9) | data formatting | bytes 9830400 | tf_op args[2]
  8.7 8.7 %copy.33.cond_hbm = bf16[128,16,1200]{2,1,0:T(8,128)(2,1)} copy(bf16[128,16,1200]{0,2,1:T(8,128)(2,1)} %param.8) | data formatting | bytes 9830400 | tf_op args[1]
  17.4 1.2 slice.19
  18.6 0.1 broadcast_in_dim.30
  18.7 0.0 slice-done
  18.7 1.4 pad_maximum_fusion.tail_ref
  20.1 0.2 pad_slice_fusion.1
  20.4 0.0 copy-start.4
  20.5 0.1 pad.8.clone
  20.5 3.0 maximum_maximum_fusion.w_hbm
  23.5 0.2 convert_reduce_fusion
  23.7 0.7 select_reduce_fusion.tab
  24.4 262.7 %shard_map.73 = (f32[4,4,4,4,2,128]{5,4,3,2,1,0:T(2,128)}, bf16[4,4,4,4,16,1280]{5,4,3,2,1,0:T(8,128)(2,1)}, bf16[4,4,4,4,16,1280]{5,4,3,2,1,0:T(8,128)(2,1)}, b...) custom-call(s32[256]{0:T(256)} %select_reduce_fusion.tab, bf16[128,16,1200]{2,1,0:T(8,128)(2,1)} %copy.32.val_hbm, ...), custom_call_target="tpu_custom_call" | custom-call | tf_op jit(solution)/shard_map/pallas_call | solution.py:291
  287.1 1.0 copy.40
  288.1 0.8 gather_fusion
  288.9 0.1 copy.34
  288.9 0.1 copy.35
  289.0 0.1 copy.36
  289.1 0.0 copy-done.1
  289.1 13.2 %all_gather.3 = bf16[16,16,1200]{2,1,0:T(8,128)(2,1)S(1)} all-gather(bf16[2,16,1200]{2,1,0:T(8,128)(2,1)S(1)} %copy-done.1), channel_id=1, replica_groups=mesh['kb'=16,'col'=8] {'col'}, dimensions={0}, use_global_device_ids=true | all-gather | bytes 691200 | tf_op jit(solution)/shard_map/all_gather | solution.py:357
  302.4 0.9 fusion
  303.3 0.3 copy.29
  303.7 0.4 mul.80
  304.1 0.7 sub.3
  (16 shorter events, 0.1 us)
Async XLA Ops:
  8.7 10.0 %slice-start = ((bf16[128,16,1200]{2,1,0:T(8,128)(2,1)}), bf16[128,16,48]{2,1,0:T(8,128)(2,1)S(1)}, s32[]{:S(2)}) async-start(bf16[128,16,1200]{2,1,0:T(8,128)(2,1)} %copy.32.val_hbm), calls=%async_computation | async-start | bytes 1048576 | tf_op jit(solution)/shard_map/slice | solution.py:347
  17.4 2.8 copy-start
  20.4 3.1 %copy-start.4 = (s32[128,1]{0,1:T(1,128)S(1)}, s32[128,1]{0,1:T(1,128)}, u32[]{:S(2)}) copy-start(s32[128,1]{0,1:T(1,128)} %param.7) | copy-start | bytes 1540
  24.4 264.7 %copy-start.1 = (bf16[2,16,1200]{2,1,0:T(8,128)(2,1)S(1)}, bf16[2,16,1200]{2,1,0:T(8,128)(2,1)}, u32[]{:S(2)}) copy-start(bf16[2,16,1200]{2,1,0:T(8,128)(2,1)} %param.10) | copy-start | bytes 230404
  24.4 278.0 %copy-start.2 = (bf16[8,16,1200]{2,1,0:T(8,128)(2,1)S(1)}, bf16[8,16,1200]{2,1,0:T(8,128)(2,1)}, u32[]{:S(2)}) copy-start(bf16[8,16,1200]{2,1,0:T(8,128)(2,1)} %param.11) | copy-start | bytes 921604
  24.4 278.0 %copy-start.3 = (f32[1200]{0:T(1024)S(1)}, f32[1200]{0:T(1024)}, u32[]{:S(2)}) copy-start(f32[1200]{0:T(1024)} %param.12) | copy-start | bytes 14404

commit v2 on v1

v2 whole, which is shorter than its diff:
```python
import functools

import jax
import jax.numpy as jnp
from jax import lax
from jax.experimental import pallas as pl
from jax.experimental.pallas import tpu as pltpu
from jax.sharding import PartitionSpec as P

MESH = pl.DeviceIdType.MESH
Z, Y, X = 0, 1, 2
ORDERS = ((X, Y, Z), (Y, Z, X), (Z, X, Y))
MAIN = 1152
TILE = 128
WIDTHS = (640, 640, 640, 512)
CUTS = ((0, 256, 512, 640), (0, 128, 384, 640), (0, 256, 384, 640), (0, 128, 256, 512))
NT = (((1,), (1,)), ((), ()))


def streams(slots, r):
    out = [(j, ORDERS[j], 0, WIDTHS[r]) for j in range(3)]
    if slots == 4:
        out += [(3, ORDERS[i], CUTS[r][i], CUTS[r][i + 1]) for i in range(3)]
    return out


def at_axis(ref, lead, axis, index, c0=None, c1=None):
    where = [slice(None)] * 3
    where[axis] = index
    return ref.at[(lead, *where, slice(None), slice(c0, c1))]


def place_kernel(
    slots,
    onehot, flag_ref, rows_hbm, cols_ref, coulomb_ref, val_hbm, cond_hbm, w_hbm,
    out_ref, ex_ref, h10, h11, h12, h13, h20, h21, h22, h23,
    vt, ct, s0, s1, s2, s3, f0, f1, f2, f3, w2, wt, st, rows, tt, zbuf, ybuf, xbuf, dbuf,
    in_sem, w_sem, row_sem, send, recv, last, local, back_send, back_recv,
):
    kb = lax.axis_index("kb")
    col = lax.axis_index("col")
    here = (kb & 3, kb >> 2, col >> 1)
    core = col & 1
    count = onehot.shape[0]
    per = 64 * 16

    def dev(chip, which):
        return (chip[Y] * 4 + chip[Z], chip[X] * 2 + which)

    def moved(axis, index):
        chip = list(here)
        chip[axis] = index
        return tuple(chip)

    load_val = pltpu.make_async_copy(val_hbm, vt, in_sem.at[0])
    load_val.start()
    load_tail = pltpu.make_async_copy(cond_hbm.at[:, MAIN:], ct, in_sem.at[1])
    load_tail.start()
    load_w = pltpu.make_async_copy(w_hbm.at[0], w2.at[core], in_sem.at[2])
    load_w.start()
    load_rows = pltpu.make_async_copy(rows_hbm, rows.at[col], in_sem.at[3])
    load_rows.start()

    barrier = pltpu.get_barrier_semaphore()
    for axis in range(3):
        for d in (1, 2, 3):
            for which in range(2):
                pl.semaphore_signal(
                    barrier, inc=1, device_id=dev(moved(axis, (here[axis] + d) & 3), which), device_id_type=MESH
                )
    pl.semaphore_signal(barrier, inc=1, device_id=dev(here, 1 - core), device_id_type=MESH)

    rounds = ((s0, h10, h20, f0), (s1, h11, h21, f1), (s2, h12, h22, f2), (s3, h13, h23, f3))
    parts = tuple(streams(slots, r) for r in range(4))
    n_streams = len(parts[0])

    def fill(buf, tile, chunk_of):
        for row in range(16):
            st[pl.ds(row, count, stride=16), :] = lax.dot_general(
                onehot[...], chunk_of(row), NT, preferred_element_type=jnp.float32
            )
        for j in range(slots):
            buf[j, :, :, :, :, pl.ds(pl.multiple_of(tile * TILE, TILE), TILE)] = (
                st[j * per : (j + 1) * per].astype(jnp.bfloat16).reshape(4, 4, 4, 16, TILE)
            )

    def build(buf, first, tiles):
        @pl.loop(0, tiles)
        def _(t):
            fill(buf, t, lambda row: vt[row, pl.ds(pl.multiple_of((first + t) * TILE, TILE), TILE), :])

    def ring(r, s, k, d):
        j, order, c0, c1 = parts[r][s]
        axis = order[k]
        there = (here[axis] + d) & 3
        return pltpu.make_async_remote_copy(
            at_axis(rounds[r][k], j, axis, there, c0, c1),
            at_axis(rounds[r][k + 1], j, axis, here[axis], c0, c1),
            send.at[r, s, k, d], recv.at[r, s, k, d],
            device_id=dev(moved(axis, there), core), device_id_type=MESH,
        )

    def keep(r, s, k):
        j, order, c0, c1 = parts[r][s]
        axis = order[k]
        return pltpu.make_async_copy(
            at_axis(rounds[r][k], j, axis, here[axis], c0, c1),
            at_axis(rounds[r][k + 1], j, axis, here[axis], c0, c1),
            local.at[r, s, k],
        )

    def start_ring(r, k):
        for d in (1, 3, 2):
            for s in range(n_streams):
                ring(r, s, k, d).start()
        for s in range(n_streams):
            keep(r, s, k).start()

    def wait_ring(r, k):
        for s in range(n_streams):
            for d in (1, 3, 2):
                c = ring(r, s, k, d)
                c.wait_send()
                c.wait_recv()
            keep(r, s, k).wait()

    def final(r, s, d):
        j, order, c0, c1 = parts[r][s]
        axis = order[2]
        there = (here[axis] + d) & 3
        lead, goal = (core, j) if j < 2 else (j, core)
        sem = last.at[r, lead, d] if j < 2 else last.at[r, s, d]
        return pltpu.make_async_remote_copy(
            at_axis(rounds[r][2], j, axis, there, c0, c1),
            at_axis(rounds[r][3], lead, axis, here[axis], c0, c1),
            send.at[r, s, 2, d], sem,
            device_id=dev(moved(axis, there), goal), device_id_type=MESH,
        )

    def final_local(r, s):
        j, order, c0, c1 = parts[r][s]
        axis = order[2]
        lead = core if j < 2 else j
        return pltpu.make_async_copy(
            at_axis(rounds[r][2], j, axis, here[axis], c0, c1),
            at_axis(rounds[r][3], lead, axis, here[axis], c0, c1),
            local.at[r, s, 2],
        )

    def start_final(r):
        for d in (1, 3, 2):
            for s in range(n_streams):
                final(r, s, d).start()
        for s in range(n_streams):
            if s < 2:
                @pl.when(core == s)
                def _():
                    final_local(r, s).start()

                @pl.when(core != s)
                def _():
                    final(r, s, 0).start()
            else:
                final_local(r, s).start()

    def wait_final(r):
        for s in range(n_streams):
            for d in (1, 3, 2):
                final(r, s, d).wait_send()
            if s < 2:
                @pl.when(core == s)
                def _():
                    final_local(r, s).wait()

                @pl.when(core != s)
                def _():
                    final(r, s, 0).wait_send()
            else:
                final_local(r, s).wait()
                for d in (1, 3, 2):
                    final(r, s, d).wait_recv()
        for mine in range(2):
            axis = ORDERS[mine][2]

            @pl.when(core == mine)
            def _():
                for lead in range(2):
                    for d in (1, 3, 2) if lead == mine else (1, 3, 2, 0):
                        at = at_axis(rounds[r][3], lead, axis, here[axis])
                        pltpu.make_async_remote_copy(
                            at, at, send.at[r, mine, 2, d], last.at[r, lead, d],
                            device_id=dev(here, 1 - core), device_id_type=MESH,
                        ).wait_recv()

    load_val.wait()
    build(s0, 0, 5)
    pl.semaphore_wait(barrier, 19)
    start_ring(0, 0)
    load_tail.wait()
    build(s1, 5, 4)
    gap = jnp.zeros((16, TILE), jnp.bfloat16)
    fill(s1, 4, lambda row: jnp.concatenate([vt[row, MAIN:, :], gap, ct[row], flag_ref[...]], axis=0))
    load_cond = pltpu.make_async_copy(cond_hbm, vt, in_sem.at[0])
    load_cond.start()
    start_ring(1, 0)

    send_w = pltpu.make_async_remote_copy(
        w_hbm.at[0], w2.at[core], w_sem.at[0], w_sem.at[1], device_id=dev(here, 1 - core), device_id_type=MESH
    )
    send_w.start()

    def row_copy(d):
        to = lax.rem(col + d, 8)
        return pltpu.make_async_remote_copy(
            rows_hbm, rows.at[col], row_sem.at[0, d], row_sem.at[1, d], device_id=(kb, to), device_id_type=MESH
        )

    for d in range(1, 8):
        row_copy(d).start()

    load_cond.wait()
    build(s2, 0, 5)
    wait_ring(0, 0)
    start_ring(0, 1)
    start_ring(2, 0)
    build(s3, 5, 4)
    wait_ring(1, 0)
    start_ring(1, 1)
    start_ring(3, 0)

    load_rows.wait()
    for d in range(1, 8):
        row_copy(d).wait()
    scaled = (cols_ref[...].astype(jnp.float32) * coulomb_ref[...][None]).astype(jnp.bfloat16)
    ex_ref[...] = lax.dot_general(
        rows[...].reshape(256, 1200), scaled.reshape(128, 1200), NT, preferred_element_type=jnp.float32
    )
    load_w.wait()
    send_w.wait()
    wt[...] = jnp.zeros_like(wt)
    for which in range(2):
        wt[which, 64:112] = w2[which, MAIN:]

    wait_ring(0, 1)
    start_final(0)
    wait_ring(2, 0)
    start_ring(2, 1)
    wait_ring(1, 1)
    start_final(1)
    wait_ring(3, 0)
    start_ring(3, 1)
    wait_ring(2, 1)
    start_final(2)
    wait_final(0)
    wait_ring(3, 1)
    start_final(3)
    wait_final(1)

    group = lax.broadcasted_iota(jnp.int32, (16, 256), 1) >> 4
    line = lax.broadcasted_iota(jnp.int32, (16, 256), 0)

    def diagonal(full):
        total = jnp.zeros((16, 256), jnp.float32)
        for i in range(16):
            total = jnp.where(group == i, full[16 * i : 16 * i + 16], total)
        return total

    def apply(i, times):
        b, z = i >> 2, i & 3
        tail = f1[b, z].reshape(256, 640)
        x = jnp.concatenate([f0[b, z].reshape(256, 640), tail], axis=1)[:, :1200]
        for n, (g0, size) in enumerate(((0, 256), (256, 256), (512, 128), (640, 256), (896, 256), (0, 0))):
            part = times(b, x, tail, g0, size).astype(jnp.bfloat16)
            if size == 0:
                s1[b, z, :, :, :, 512:640] = part.reshape(4, 4, 16, 128)
                tt[b, z] = diagonal(lax.dot_general(tail[:, 512:], part, NT, preferred_element_type=jnp.float32))
            else:
                to, at = (s0, g0) if g0 < 640 else (s1, g0 - 640)
                to[b, z, :, :, :, at : at + size] = part.reshape(4, 4, 16, size)

    def one(which, x, g0, size):
        w = w2[which, g0 : g0 + size, :] if size else wt[which]
        return lax.dot_general(x, w, NT, preferred_element_type=jnp.float32)

    fixed = 8 if slots == 3 else 16

    @pl.loop(0, fixed)
    def _(i):
        apply(i, lambda b, x, tail, g0, size: one(jnp.where(b < 2, core, b - 2), x, g0, size))

    if slots == 3:
        def either(b, x, tail, g0, size):
            flag = tail[:, 624:625].astype(jnp.float32) > 0.5
            return jnp.where(flag, one(1, x, g0, size), one(0, x, g0, size))

        @pl.loop(8, 12)
        def _(i):
            apply(i, either)

    wait_final(2)

    @pl.loop(0, 4 * slots)
    def _(i):
        b, z = i >> 2, i & 3
        full = lax.dot_general(
            f2[b, z].reshape(256, 640), s0[b, z].reshape(256, 640), NT, preferred_element_type=jnp.float32
        )
        tt[b, z] = tt[b, z] + diagonal(full)

    wait_final(3)

    @pl.loop(0, 4 * slots)
    def _(i):
        b, z = i >> 2, i & 3
        full = lax.dot_general(
            f3[b, z].reshape(256, 512),
            s1[b, z, :, :, :, :512].reshape(256, 512),
            NT,
            preferred_element_type=jnp.float32,
        )
        got = diagonal(full) + tt[b, z]
        turned = jnp.where(group == line, got, 0.0)
        for k in range(1, 16):
            shifted = pltpu.roll(pltpu.roll(got, 16 - k, 0), 16 * k, 1)
            turned = jnp.where(group == ((line + k) & 15), shifted, turned)
        for slot in range(16):
            zbuf[b, z, slot >> 2, slot & 3, 0:1] = turned[slot : slot + 1, :128]
            zbuf[b, z, slot >> 2, slot & 3, 1:2] = turned[slot : slot + 1, 128:]
        back_core = jnp.where(b < 2, b, core)
        mine = (z == here[Z]) & (back_core == core)
        src = zbuf.at[b, z]
        dst = ybuf.at[jnp.where(b < 2, core, b), here[Z]]

        @pl.when(mine)
        def _():
            pltpu.make_async_copy(src, dst, back_recv.at[0]).start()

        @pl.when(jnp.logical_not(mine))
        def _():
            pltpu.make_async_remote_copy(
                src, dst, back_send.at[0], back_recv.at[0],
                device_id=dev(moved(Z, z), back_core), device_id_type=MESH,
            ).start()

    pltpu.make_async_copy(ybuf, ybuf, back_recv.at[0]).wait()

    def back(j, k, d):
        axis = ((Y, X) if j < 2 else (X, Y))[k]
        src, dst = ((ybuf, xbuf), (xbuf, dbuf))[k]
        there = (here[axis] + d) & 3
        return pltpu.make_async_remote_copy(
            at_axis(src, j, axis, there), at_axis(dst, j, axis, here[axis]),
            back_send.at[1 + 16 * k + 4 * j + d], back_recv.at[1 + 16 * k + 4 * j + d],
            device_id=dev(moved(axis, there), core), device_id_type=MESH,
        )

    def back_keep(j, k):
        axis = ((Y, X) if j < 2 else (X, Y))[k]
        src, dst = ((ybuf, xbuf), (xbuf, dbuf))[k]
        return pltpu.make_async_copy(
            at_axis(src, j, axis, here[axis]), at_axis(dst, j, axis, here[axis]), back_recv.at[1 + 16 * k + 4 * j]
        )

    for k in range(2):
        for d in (2, 1, 3):
            for j in range(slots):
                back(j, k, d).start()
        for j in range(slots):
            back_keep(j, k).start()
        for j in range(slots):
            back_keep(j, k).wait()
            for d in (1, 3, 2):
                back(j, k, d).wait()

    @pl.loop(0, 4 * slots - (slots - 1))
    def _(_):
        pltpu.make_async_copy(zbuf.at[0, 0], zbuf.at[0, 0], back_send.at[0]).wait()

    out_ref[...] = dbuf[...]


def direct_terms(slots, onehot, flags, row_vc, col_vc, coulomb, val_t, cond_t, screened):
    hbm = pl.BlockSpec(memory_space=pl.ANY)
    vmem = pl.BlockSpec(memory_space=pltpu.VMEM)
    bf16 = jnp.bfloat16
    wide = [(slots, 4, 4, 4, 16, w) for w in WIDTHS]
    small = (slots, 4, 4, 4, 2, 128)
    f32 = jnp.float32
    dma = pltpu.SemaphoreType.DMA
    out = pl.pallas_call(
        functools.partial(place_kernel, slots),
        out_shape=(
            jax.ShapeDtypeStruct(small, f32),
            jax.ShapeDtypeStruct((256, 128), f32),
            *(jax.ShapeDtypeStruct(w, bf16) for w in wide),
            *(jax.ShapeDtypeStruct(w, bf16) for w in wide),
        ),
        in_specs=[vmem, vmem, hbm, vmem, vmem, hbm, hbm, hbm],
        out_specs=(vmem, vmem) + (hbm,) * 8,
        scratch_shapes=[
            pltpu.VMEM(val_t.shape, bf16),
            pltpu.VMEM((16, 48, 128), bf16),
            *(pltpu.VMEM(w, bf16) for w in wide),
            *(pltpu.VMEM(w, bf16) for w in wide),
            pltpu.VMEM((2, 1200, 1200), bf16),
            pltpu.VMEM((2, TILE, 1200), bf16),
            pltpu.VMEM((slots * 64 * 16, TILE), f32),
            pltpu.VMEM((8, 2, 16, 1200), bf16),
            pltpu.VMEM((slots, 4, 16, 256), f32),
            *(pltpu.VMEM(small, f32) for _ in range(4)),
            dma((4,)),
            dma((2,)),
            dma((2, 8)),
            dma((4, 6, 3, 4)),
            dma((4, 6, 2, 4)),
            dma((4, 6, 4)),
            dma((4, 6, 3)),
            dma((33,)),
            dma((33,)),
        ],
        compiler_params=pltpu.CompilerParams(
            collective_id=slots, has_side_effects=True, vmem_limit_bytes=61 * 2**20
        ),
    )(onehot, flags, row_vc, col_vc, coulomb, val_t, cond_t, screened)
    return out[0].reshape(slots * 64, 256), out[1]


def shards(q_index, cond_pairs, val_pairs, row_vc, col_vc, coulomb, screened):
    count = cond_pairs.shape[0]
    slots = 4
    target = q_index[:, 0]
    same = target[:, None] == target[None, :]
    earlier = jnp.arange(count)[None, :] < jnp.arange(count)[:, None]
    rank = jnp.sum((same & earlier).astype(jnp.int32), axis=1)
    core, x, z, y = target & 1, (target >> 1) & 3, (target >> 3) & 3, (target >> 5) & 3
    chip = (z * 4 + y) * 4 + x
    place = (rank * 2 + core) * 64 + chip
    spots = jnp.arange(slots * 64, dtype=jnp.int32)
    onehot = (place[None, :] == spots[:, None]).astype(jnp.bfloat16)
    flags = jnp.broadcast_to(core.astype(jnp.bfloat16)[None, :], (16, count))
    direct, exchange = direct_terms(
        slots, onehot, flags, row_vc, col_vc, coulomb[None, :],
        val_pairs.transpose(1, 2, 0), cond_pairs.transpose(1, 2, 0), screened,
    )
    direct = direct[place].reshape(count, 4, 4, 4, 4).transpose(0, 3, 1, 4, 2).reshape(count, 256)
    exchange = exchange.reshape(16, 16, 8, 16).transpose(0, 2, 1, 3).reshape(count, 256)
    return 2.0 * exchange - direct


def solution(mesh):
    return jax.shard_map(
        shards,
        mesh=mesh,
        in_specs=(
            P(("kb", "col"), None),
            P(("kb", "col"), None, None),
            P(("kb", "col"), None, None),
            P(("kb", "col"), None, None),
            P("col", None, None),
            P(),
            P(("kb", "col"), None, None),
        ),
        out_specs=P(("kb", "col"), None),
        check_vma=False,
    )
```

time: 307 us -> 270 us (0.88)
  local copies, waits for them, and re-layouts: 21.8 us -> 4.78 us
  blocking collectives: 13.2 us -> 0 us
    unnamed x13 -> x3, local copies, waits for them, and re-layouts: 18.4 us -> 0.97 us
    all_gather x1 -> x0, blocking collectives: 13.2 us -> none  [shards(): lax.all_gather(row_vc, 'col', axis=0, tiled=True)]
    concatenate x2 -> x0, other arithmetic: 4.43 us -> none  [the longest x1 3 us: shards(): jnp.concatenate([w[:MAIN], jnp.zeros((64, WIDE), jnp.bfloat16), w[MAIN:],...]
where the time goes in v2:
time: 270 us; the launch traced here: 269 us
  Pallas kernels  261 us (97%)
  local copies, waits for them, and re-layouts  4.78 us (2%)
  other arithmetic  3.83 us (1%)
    pallas_call x1, Pallas kernels, direct_terms(): pl.pallas_call(functools.partial(place_kernel, slots), out_shape=(jax.Sha...  261 us

profile of v2, /device:TPU:0, one launch (start us, length us, event | category | flops | bytes accessed | tf_op | source)
XLA Modules:
  0.0 269.3 jit_solution(7947683575123796373)
XLA Ops:
  0.0 0.9 convert_reduce_fusion
  0.9 0.7 and_convert_fusion
  1.6 0.7 fusion.onehot
  2.2 0.6 broadcast_in_dim.4.flag_ref
  2.8 1.3 broadcast_in_dim.5.coulomb_ref
  4.1 0.0 copy-start
  4.1 260.7 %shard_map.73 = (f32[4,4,4,4,2,128]{5,4,3,2,1,0:T(2,128)}, f32[256,128]{1,0:T(8,128)}, bf16[4,4,4,4,16,640]{5,4,3,2,1,0:T(8,128)(2,1)}, bf16[4,4,4,4,16,640]{5,4...) custom-call(bf16[256,128]{1,0:T(8,128)(2,1)} %fusion.onehot, ...), custom_call_target="tpu_custom_call" | custom-call | tf_op jit(solution)/shard_map/pallas_call | solution.py:390
  264.8 1.0 copy.26
  265.7 0.0 copy-done
  265.8 0.8 gather_fusion
  266.5 0.1 copy.19
  266.6 0.1 copy.20
  266.7 0.1 copy.21
  266.8 0.9 broadcast_multiply_fusion
  267.7 0.3 mul.78
  268.0 0.2 copy.25
  268.2 0.4 mul.80
  268.7 0.7 sub.3
  (2 shorter events, 0.0 us)
Async XLA Ops:
  4.1 261.6 %copy-start = (s32[128,1]{0,1:T(1,128)S(1)}, s32[128,1]{0,1:T(1,128)}, u32[]{:S(2)}) copy-start(s32[128,1]{0,1:T(1,128)} %param.7) | copy-start | bytes 1540

commit v3 on v2

--- a/solution.py
+++ b/solution.py
@@ -30,19 +30,210 @@
     return ref.at[(lead, *where, slice(None), slice(c0, c1))]
 
 
+def fill_slots(buf, st, onehot, slots, tile, chunk_of):
+    per = 64 * 16
+    for row in range(16):
+        st[pl.ds(row, 64 * slots, stride=16), :] = lax.dot_general(
+            onehot[: 64 * slots, :], chunk_of(row), NT, preferred_element_type=jnp.float32
+        )
+    for j in range(slots):
+        buf[j, :, :, :, :, pl.ds(pl.multiple_of(tile * TILE, TILE), TILE)] = (
+            st[j * per : (j + 1) * per].astype(jnp.bfloat16).reshape(4, 4, 4, 16, TILE)
+        )
+
+
+def prepare_kernel(
+    q_ref, val_hbm, cond_hbm, rows_hbm,
+    onehot, flag_ref, place_ref, crowd_ref, h10, extra_hbm, s1_hbm, rows_out,
+    vt, ct, s0, s1, st, votes, sums, in_sem, row_sem, one_sem, two_sem, send, recv,
+):
+    kb = lax.axis_index("kb")
+    col = lax.axis_index("col")
+    here = (kb & 3, kb >> 2, col >> 1)
+    load_val = pltpu.make_async_copy(val_hbm, vt, in_sem.at[0])
+    load_val.start()
+    load_tail = pltpu.make_async_copy(cond_hbm.at[:, MAIN:], ct, in_sem.at[2])
+    load_tail.start()
+    own_rows = pltpu.make_async_copy(rows_hbm, rows_out.at[col], in_sem.at[1])
+    own_rows.start()
+
+    def mate(d):
+        return (kb, (col + d) & 7)
+
+    def far(d):
+        return ((kb + d) & 15, col)
+
+    barrier = pltpu.get_barrier_semaphore()
+    for d in range(1, 8):
+        pl.semaphore_signal(barrier, inc=1, device_id=mate(d), device_id_type=MESH)
+    for d in range(1, 16):
+        pl.semaphore_signal(barrier, inc=1, device_id=far(d), device_id_type=MESH)
+
+    size = q_ref.shape[1]
+    along = jnp.broadcast_to(q_ref[...], (size, size))
+    before = lax.broadcasted_iota(jnp.int32, (size, size), 0) < lax.broadcasted_iota(jnp.int32, (size, size), 1)
+
+    def turned(a):
+        return jnp.transpose(a.astype(jnp.float32)).astype(jnp.int32)
+
+    down = turned(along)
+    repeat = jnp.sum(jnp.where((along == down) & before, 1.0, 0.0), axis=0, keepdims=True)
+    repeats = jnp.broadcast_to(repeat, (size, size)).astype(jnp.int32)
+    both = ((along >> 1) == (down >> 1)) & before & (repeats > 0) & (turned(repeats) > 0)
+    more = jnp.sum(jnp.where(both, 1.0, 0.0), axis=0, keepdims=True)
+    q = q_ref[...]
+    core, x, z, y = q & 1, (q >> 1) & 3, (q >> 3) & 3, (q >> 5) & 3
+    chip = (z * 4 + y) * 4 + x
+    slot = jnp.where(repeat > 0.5, 2 + more.astype(jnp.int32), core)
+    place = slot * 64 + chip
+    place_ref[...] = slot + ((((y * 4 + x) * 4) + z) << 2)
+    flag_ref[...] = jnp.broadcast_to(core.astype(jnp.float32), (16, size)).astype(jnp.bfloat16)
+    spots = lax.broadcasted_iota(jnp.int32, onehot.shape, 0)
+    onehot[...] = jnp.where(spots == place, 1.0, 0.0).astype(jnp.bfloat16)
+    votes[0] = jnp.broadcast_to(jnp.max(more, axis=1, keepdims=True), (8, TILE))
+
+    pl.semaphore_wait(barrier, 22)
+
+    def first(d):
+        return pltpu.make_async_remote_copy(
+            votes.at[0], votes.at[d], one_sem.at[0, d], one_sem.at[1, d], device_id=mate(d), device_id_type=MESH
+        )
+
+    def second(d):
+        return pltpu.make_async_remote_copy(
+            sums.at[0], sums.at[d], two_sem.at[0, d], two_sem.at[1, d], device_id=far(d), device_id_type=MESH
+        )
+
+    def row_copy(d):
+        return pltpu.make_async_remote_copy(
+            rows_hbm, rows_out.at[col], row_sem.at[0, d], row_sem.at[1, d], device_id=mate(d), device_id_type=MESH
+        )
+
+    for d in range(1, 8):
+        first(d).start()
+    for d in range(1, 8):
+        row_copy(d).start()
+
+    load_val.wait()
+
+    def ring(part, j, d):
+        c0, c1 = ((0, 256), (256, 640))[part]
+        axis = ORDERS[j][0]
+        chip = list(here)
+        chip[axis] = (here[axis] + d) & 3
+        return pltpu.make_async_remote_copy(
+            at_axis(s0, j, axis, chip[axis], c0, c1), at_axis(h10, j, axis, here[axis], c0, c1),
+            send.at[part, j, d], recv.at[part, j, d],
+            device_id=(chip[Y] * 4 + chip[Z], chip[X] * 2 + (col & 1)), device_id_type=MESH,
+        )
+
+    def keep(j):
+        axis = ORDERS[j][0]
+        return pltpu.make_async_copy(
+            at_axis(s0, j, axis, here[axis]), at_axis(h10, j, axis, here[axis]), recv.at[0, j, 0]
+        )
+
+    for part, (lo, hi) in enumerate(((0, 2), (2, 5))):
+        @pl.loop(lo, hi)
+        def _(t):
+            fill_slots(s0, st, onehot, 4, t, lambda row: vt[row, pl.ds(pl.multiple_of(t * TILE, TILE), TILE), :])
+
+        if part == 1:
+            for d in range(1, 8):
+                first(d).wait()
+            sums[0] = jnp.max(votes[...], axis=0)
+            for d in range(1, 16):
+                second(d).start()
+        for d in (1, 3, 2):
+            for j in range(3):
+                ring(part, j, d).start()
+    for j in range(3):
+        keep(j).start()
+    store_extra = pltpu.make_async_copy(s0.at[3], extra_hbm.at[0], in_sem.at[3])
+    store_extra.start()
+
+    @pl.loop(0, 4)
+    def _(t):
+        fill_slots(
+            s1, st, onehot, 4, t, lambda row: vt[row, pl.ds(pl.multiple_of(640 + t * TILE, TILE), TILE), :]
+        )
+
+    load_tail.wait()
+    gap = jnp.zeros((16, TILE), jnp.bfloat16)
+    fill_slots(
+        s1, st, onehot, 4, 4,
+        lambda row: jnp.concatenate([vt[row, MAIN:, :], gap, ct[row], flag_ref[...]], axis=0),
+    )
+    store = pltpu.make_async_copy(s1, s1_hbm, in_sem.at[4])
+    store.start()
+    for d in range(1, 16):
+        second(d).wait()
+    crowd_ref[...] = jnp.max(sums[...], axis=0)
+    own_rows.wait()
+    for d in range(1, 8):
+        row_copy(d).wait()
+    store_extra.wait()
+    store.wait()
+    for j in range(3):
+        for d in (1, 3, 2):
+            for part in range(2):
+                ring(part, j, d).wait()
+        keep(j).wait()
+
+
+def prepare(q_row, val_t, cond_t, row_vc):
+    hbm = pl.BlockSpec(memory_space=pl.ANY)
+    vmem = pl.BlockSpec(memory_space=pltpu.VMEM)
+    bf16, f32 = jnp.bfloat16, jnp.float32
+    count = q_row.shape[1]
+    first = (4, 4, 4, 4, 16, WIDTHS[0])
+    dma = pltpu.SemaphoreType.DMA
+    return pl.pallas_call(
+        prepare_kernel,
+        out_shape=(
+            jax.ShapeDtypeStruct((256, count), bf16),
+            jax.ShapeDtypeStruct((16, count), bf16),
+            jax.ShapeDtypeStruct((1, count), jnp.int32),
+            jax.ShapeDtypeStruct((8, TILE), f32),
+            jax.ShapeDtypeStruct((3,) + first[1:], bf16),
+            jax.ShapeDtypeStruct((1,) + first[1:], bf16),
+            jax.ShapeDtypeStruct(first, bf16),
+            jax.ShapeDtypeStruct((8,) + row_vc.shape, bf16),
+        ),
+        in_specs=[vmem, hbm, hbm, hbm],
+        out_specs=(vmem, vmem, vmem, vmem, hbm, hbm, hbm, hbm),
+        scratch_shapes=[
+            pltpu.VMEM(val_t.shape, bf16),
+            pltpu.VMEM((16, val_t.shape[1] - MAIN, count), bf16),
+            pltpu.VMEM(first, bf16),
+            pltpu.VMEM(first, bf16),
+            pltpu.VMEM((256 * 16, TILE), f32),
+            pltpu.VMEM((8, 8, TILE), f32),
+            pltpu.VMEM((16, 8, TILE), f32),
+            dma((5,)),
+            dma((2, 8)),
+            dma((2, 8)),
+            dma((2, 16)),
+            dma((2, 3, 4)),
+            dma((2, 3, 4)),
+        ],
+        compiler_params=pltpu.CompilerParams(
+            collective_id=1, has_side_effects=True, vmem_limit_bytes=48 * 2**20
+        ),
+    )(q_row, val_t, cond_t, row_vc)
+
+
 def place_kernel(
     slots,
-    onehot, flag_ref, rows_hbm, cols_ref, coulomb_ref, val_hbm, cond_hbm, w_hbm,
-    out_ref, ex_ref, h10, h11, h12, h13, h20, h21, h22, h23,
-    vt, ct, s0, s1, s2, s3, f0, f1, f2, f3, w2, wt, st, rows, tt, zbuf, ybuf, xbuf, dbuf,
-    in_sem, w_sem, row_sem, send, recv, last, local, back_send, back_recv,
+    onehot, rows_hbm, cols_ref, coulomb_ref, h10, extra_hbm, s1_hbm, cond_hbm, w_hbm,
+    out_ref, ex_ref, h10x, h11, h12, h13, h20, h21, h22, h23,
+    vt, bounce, s0, s1, s2, s3, f0, f1, f2, f3, w2, wt, st, rows, tt, zbuf, ybuf, dbuf,
+    in_sem, w_sem, send, recv, last, local, local_on, back_send, back_recv,
 ):
     kb = lax.axis_index("kb")
     col = lax.axis_index("col")
     here = (kb & 3, kb >> 2, col >> 1)
     core = col & 1
-    count = onehot.shape[0]
-    per = 64 * 16
 
     def dev(chip, which):
         return (chip[Y] * 4 + chip[Z], chip[X] * 2 + which)
@@ -52,13 +243,11 @@
         chip[axis] = index
         return tuple(chip)
 
-    load_val = pltpu.make_async_copy(val_hbm, vt, in_sem.at[0])
-    load_val.start()
-    load_tail = pltpu.make_async_copy(cond_hbm.at[:, MAIN:], ct, in_sem.at[1])
-    load_tail.start()
+    load_cond = pltpu.make_async_copy(cond_hbm.at[:, :MAIN], vt, in_sem.at[0])
+    load_cond.start()
     load_w = pltpu.make_async_copy(w_hbm.at[0], w2.at[core], in_sem.at[2])
     load_w.start()
-    load_rows = pltpu.make_async_copy(rows_hbm, rows.at[col], in_sem.at[3])
+    load_rows = pltpu.make_async_copy(rows_hbm, rows, in_sem.at[3])
     load_rows.start()
 
     barrier = pltpu.get_barrier_semaphore()
@@ -70,32 +259,34 @@
                 )
     pl.semaphore_signal(barrier, inc=1, device_id=dev(here, 1 - core), device_id_type=MESH)
 
-    rounds = ((s0, h10, h20, f0), (s1, h11, h21, f1), (s2, h12, h22, f2), (s3, h13, h23, f3))
+    def across(dy, dx):
+        return (here[Z], (here[Y] + dy) & 3, (here[X] + dx) & 3)
+
+    for dy in (1, 2, 3):
+        for dx in (1, 2, 3):
+            pl.semaphore_signal(barrier, inc=1, device_id=dev(across(dy, dx), core), device_id_type=MESH)
+
+    rounds = ((extra_hbm, h10x, h20, f0), (s1_hbm, h11, h21, f1), (s2, h12, h22, f2), (s3, h13, h23, f3))
     parts = tuple(streams(slots, r) for r in range(4))
     n_streams = len(parts[0])
-
-    def fill(buf, tile, chunk_of):
-        for row in range(16):
-            st[pl.ds(row, count, stride=16), :] = lax.dot_general(
-                onehot[...], chunk_of(row), NT, preferred_element_type=jnp.float32
-            )
-        for j in range(slots):
-            buf[j, :, :, :, :, pl.ds(pl.multiple_of(tile * TILE, TILE), TILE)] = (
-                st[j * per : (j + 1) * per].astype(jnp.bfloat16).reshape(4, 4, 4, 16, TILE)
-            )
 
     def build(buf, first, tiles):
         @pl.loop(0, tiles)
         def _(t):
-            fill(buf, t, lambda row: vt[row, pl.ds(pl.multiple_of((first + t) * TILE, TILE), TILE), :])
+            fill_slots(buf, st, onehot, slots, t, lambda row: vt[row, pl.ds(pl.multiple_of((first + t) * TILE, TILE), TILE), :])
+
+    def held(r, j, k):
+        if r == 0 and k < 2:
+            return (h10, j) if j < 3 else (rounds[0][k], 0)
+        return rounds[r][k], j
 
     def ring(r, s, k, d):
         j, order, c0, c1 = parts[r][s]
         axis = order[k]
         there = (here[axis] + d) & 3
         return pltpu.make_async_remote_copy(
-            at_axis(rounds[r][k], j, axis, there, c0, c1),
-            at_axis(rounds[r][k + 1], j, axis, here[axis], c0, c1),
+            at_axis(*held(r, j, k), axis, there, c0, c1),
+            at_axis(*held(r, j, k + 1), axis, here[axis], c0, c1),
             send.at[r, s, k, d], recv.at[r, s, k, d],
             device_id=dev(moved(axis, there), core), device_id_type=MESH,
         )
@@ -103,26 +294,37 @@
     def keep(r, s, k):
         j, order, c0, c1 = parts[r][s]
         axis = order[k]
-        return pltpu.make_async_copy(
-            at_axis(rounds[r][k], j, axis, here[axis], c0, c1),
-            at_axis(rounds[r][k + 1], j, axis, here[axis], c0, c1),
-            local.at[r, s, k],
-        )
-
-    def start_ring(r, k):
+        src = at_axis(*held(r, j, k), axis, here[axis], c0, c1)
+        dst = at_axis(*held(r, j, k + 1), axis, here[axis], c0, c1)
+        if k == 0 and r > 1:
+            return (pltpu.make_async_copy(src, dst, local.at[r, s, k]),)
+        via = bounce.at[r % 2, j, :, :, :, c0:c1]
+        return (
+            pltpu.make_async_copy(src, via, local.at[r, s, k]),
+            pltpu.make_async_copy(via, dst, local_on.at[r, s, k]),
+        )
+
+    def start_ring(r, k, lo=0, hi=n_streams):
         for d in (1, 3, 2):
-            for s in range(n_streams):
+            for s in range(lo, hi):
                 ring(r, s, k, d).start()
-        for s in range(n_streams):
-            keep(r, s, k).start()
-
-    def wait_ring(r, k):
-        for s in range(n_streams):
+        for s in range(lo, hi):
+            keep(r, s, k)[0].start()
+
+    def wait_ring(r, k, lo=0, hi=n_streams):
+        for s in range(lo, hi):
+            own = keep(r, s, k)
+            own[0].wait()
+            if len(own) > 1:
+                own[1].start()
+        for s in range(lo, hi):
             for d in (1, 3, 2):
                 c = ring(r, s, k, d)
                 c.wait_send()
                 c.wait_recv()
-            keep(r, s, k).wait()
+            own = keep(r, s, k)
+            if len(own) > 1:
+                own[1].wait()
 
     def final(r, s, d):
         j, order, c0, c1 = parts[r][s]
@@ -192,36 +394,18 @@
                             device_id=dev(here, 1 - core), device_id_type=MESH,
                         ).wait_recv()
 
-    load_val.wait()
-    build(s0, 0, 5)
-    pl.semaphore_wait(barrier, 19)
-    start_ring(0, 0)
-    load_tail.wait()
-    build(s1, 5, 4)
-    gap = jnp.zeros((16, TILE), jnp.bfloat16)
-    fill(s1, 4, lambda row: jnp.concatenate([vt[row, MAIN:, :], gap, ct[row], flag_ref[...]], axis=0))
-    load_cond = pltpu.make_async_copy(cond_hbm, vt, in_sem.at[0])
-    load_cond.start()
+    pl.semaphore_wait(barrier, 28)
+    start_ring(0, 1, 0, 3)
+    start_ring(0, 0, 3)
     start_ring(1, 0)
-
     send_w = pltpu.make_async_remote_copy(
         w_hbm.at[0], w2.at[core], w_sem.at[0], w_sem.at[1], device_id=dev(here, 1 - core), device_id_type=MESH
     )
     send_w.start()
-
-    def row_copy(d):
-        to = lax.rem(col + d, 8)
-        return pltpu.make_async_remote_copy(
-            rows_hbm, rows.at[col], row_sem.at[0, d], row_sem.at[1, d], device_id=(kb, to), device_id_type=MESH
-        )
-
-    for d in range(1, 8):
-        row_copy(d).start()
-
     load_cond.wait()
     build(s2, 0, 5)
-    wait_ring(0, 0)
-    start_ring(0, 1)
+    wait_ring(0, 0, 3)
+    start_ring(0, 1, 3)
     start_ring(2, 0)
     build(s3, 5, 4)
     wait_ring(1, 0)
@@ -229,8 +413,6 @@
     start_ring(3, 0)
 
     load_rows.wait()
-    for d in range(1, 8):
-        row_copy(d).wait()
     scaled = (cols_ref[...].astype(jnp.float32) * coulomb_ref[...][None]).astype(jnp.bfloat16)
     ex_ref[...] = lax.dot_general(
         rows[...].reshape(256, 1200), scaled.reshape(128, 1200), NT, preferred_element_type=jnp.float32
@@ -282,20 +464,17 @@
         w = w2[which, g0 : g0 + size, :] if size else wt[which]
         return lax.dot_general(x, w, NT, preferred_element_type=jnp.float32)
 
-    fixed = 8 if slots == 3 else 16
-
-    @pl.loop(0, fixed)
+    @pl.loop(0, 8)
     def _(i):
-        apply(i, lambda b, x, tail, g0, size: one(jnp.where(b < 2, core, b - 2), x, g0, size))
-
-    if slots == 3:
-        def either(b, x, tail, g0, size):
-            flag = tail[:, 624:625].astype(jnp.float32) > 0.5
-            return jnp.where(flag, one(1, x, g0, size), one(0, x, g0, size))
-
-        @pl.loop(8, 12)
-        def _(i):
-            apply(i, either)
+        apply(i, lambda b, x, tail, g0, size: one(core, x, g0, size))
+
+    def either(b, x, tail, g0, size):
+        flag = tail[:, 624:625].astype(jnp.float32) > 0.5
+        return jnp.where(flag, one(1, x, g0, size), one(0, x, g0, size))
+
+    @pl.loop(8, 4 * slots)
+    def _(i):
+        apply(i, either)
 
     wait_final(2)
 
@@ -329,7 +508,7 @@
         back_core = jnp.where(b < 2, b, core)
         mine = (z == here[Z]) & (back_core == core)
         src = zbuf.at[b, z]
-        dst = ybuf.at[jnp.where(b < 2, core, b), here[Z]]
+        dst = ybuf.at[:, :, jnp.where(b < 2, core, b), here[Z]]
 
         @pl.when(mine)
         def _():
@@ -343,34 +522,23 @@
             ).start()
 
     pltpu.make_async_copy(ybuf, ybuf, back_recv.at[0]).wait()
-
-    def back(j, k, d):
-        axis = ((Y, X) if j < 2 else (X, Y))[k]
-        src, dst = ((ybuf, xbuf), (xbuf, dbuf))[k]
-        there = (here[axis] + d) & 3
+    back_own = pltpu.make_async_copy(ybuf.at[here[Y], here[X]], dbuf.at[here[Y], here[X]], back_recv.at[16])
+    back_own.start()
+
+    def back(dy, dx):
+        chip = across(dy, dx)
         return pltpu.make_async_remote_copy(
-            at_axis(src, j, axis, there), at_axis(dst, j, axis, here[axis]),
-            back_send.at[1 + 16 * k + 4 * j + d], back_recv.at[1 + 16 * k + 4 * j + d],
-            device_id=dev(moved(axis, there), core), device_id_type=MESH,
-        )
-
-    def back_keep(j, k):
-        axis = ((Y, X) if j < 2 else (X, Y))[k]
-        src, dst = ((ybuf, xbuf), (xbuf, dbuf))[k]
-        return pltpu.make_async_copy(
-            at_axis(src, j, axis, here[axis]), at_axis(dst, j, axis, here[axis]), back_recv.at[1 + 16 * k + 4 * j]
-        )
-
-    for k in range(2):
-        for d in (2, 1, 3):
-            for j in range(slots):
-                back(j, k, d).start()
-        for j in range(slots):
-            back_keep(j, k).start()
-        for j in range(slots):
-            back_keep(j, k).wait()
-            for d in (1, 3, 2):
-                back(j, k, d).wait()
+            ybuf.at[chip[Y], chip[X]], dbuf.at[here[Y], here[X]],
+            back_send.at[4 * dy + dx], back_recv.at[4 * dy + dx],
+            device_id=dev(chip, core), device_id_type=MESH,
+        )
+
+    ways = [(dy, dx) for dy in (2, 1, 3, 0) for dx in (2, 1, 3, 0) if dy or dx]
+    for way in ways:
+        back(*way).start()
+    back_own.wait()
+    for way in ways:
+        back(*way).wait()
 
     @pl.loop(0, 4 * slots - (slots - 1))
     def _(_):
@@ -379,70 +547,70 @@
     out_ref[...] = dbuf[...]
 
 
-def direct_terms(slots, onehot, flags, row_vc, col_vc, coulomb, val_t, cond_t, screened):
+def direct_terms(slots, onehot, rows, col_vc, coulomb, h10, extra, second, cond_t, screened):
     hbm = pl.BlockSpec(memory_space=pl.ANY)
     vmem = pl.BlockSpec(memory_space=pltpu.VMEM)
-    bf16 = jnp.bfloat16
+    bf16, f32 = jnp.bfloat16, jnp.float32
     wide = [(slots, 4, 4, 4, 16, w) for w in WIDTHS]
-    small = (slots, 4, 4, 4, 2, 128)
-    f32 = jnp.float32
+    back = (4, 4, slots, 4, 2, 128)
     dma = pltpu.SemaphoreType.DMA
     out = pl.pallas_call(
         functools.partial(place_kernel, slots),
         out_shape=(
-            jax.ShapeDtypeStruct(small, f32),
+            jax.ShapeDtypeStruct(back, f32),
             jax.ShapeDtypeStruct((256, 128), f32),
-            *(jax.ShapeDtypeStruct(w, bf16) for w in wide),
+            jax.ShapeDtypeStruct(extra.shape, bf16),
+            *(jax.ShapeDtypeStruct(w, bf16) for w in wide[1:]),
             *(jax.ShapeDtypeStruct(w, bf16) for w in wide),
         ),
-        in_specs=[vmem, vmem, hbm, vmem, vmem, hbm, hbm, hbm],
+        in_specs=[vmem, hbm, vmem, vmem, hbm, hbm, hbm, hbm, hbm],
         out_specs=(vmem, vmem) + (hbm,) * 8,
         scratch_shapes=[
-            pltpu.VMEM(val_t.shape, bf16),
-            pltpu.VMEM((16, 48, 128), bf16),
+            pltpu.VMEM((16, MAIN, cond_t.shape[2]), bf16),
+            pltpu.VMEM((2, slots, 4, 4, 16, WIDTHS[0]), bf16),
             *(pltpu.VMEM(w, bf16) for w in wide),
             *(pltpu.VMEM(w, bf16) for w in wide),
             pltpu.VMEM((2, 1200, 1200), bf16),
             pltpu.VMEM((2, TILE, 1200), bf16),
             pltpu.VMEM((slots * 64 * 16, TILE), f32),
-            pltpu.VMEM((8, 2, 16, 1200), bf16),
+            pltpu.VMEM(rows.shape, bf16),
             pltpu.VMEM((slots, 4, 16, 256), f32),
-            *(pltpu.VMEM(small, f32) for _ in range(4)),
+            pltpu.VMEM((slots, 4, 4, 4, 2, 128), f32),
+            pltpu.VMEM(back, f32),
+            pltpu.VMEM(back, f32),
             dma((4,)),
             dma((2,)),
-            dma((2, 8)),
             dma((4, 6, 3, 4)),
             dma((4, 6, 2, 4)),
             dma((4, 6, 4)),
             dma((4, 6, 3)),
-            dma((33,)),
-            dma((33,)),
+            dma((4, 6, 3)),
+            dma((17,)),
+            dma((17,)),
         ],
         compiler_params=pltpu.CompilerParams(
             collective_id=slots, has_side_effects=True, vmem_limit_bytes=61 * 2**20
         ),
-    )(onehot, flags, row_vc, col_vc, coulomb, val_t, cond_t, screened)
+    )(onehot, rows, col_vc, coulomb, h10, extra, second, cond_t, screened)
     return out[0].reshape(slots * 64, 256), out[1]
 
 
 def shards(q_index, cond_pairs, val_pairs, row_vc, col_vc, coulomb, screened):
     count = cond_pairs.shape[0]
-    slots = 4
-    target = q_index[:, 0]
-    same = target[:, None] == target[None, :]
-    earlier = jnp.arange(count)[None, :] < jnp.arange(count)[:, None]
-    rank = jnp.sum((same & earlier).astype(jnp.int32), axis=1)
-    core, x, z, y = target & 1, (target >> 1) & 3, (target >> 3) & 3, (target >> 5) & 3
-    chip = (z * 4 + y) * 4 + x
-    place = (rank * 2 + core) * 64 + chip
-    spots = jnp.arange(slots * 64, dtype=jnp.int32)
-    onehot = (place[None, :] == spots[:, None]).astype(jnp.bfloat16)
-    flags = jnp.broadcast_to(core.astype(jnp.bfloat16)[None, :], (16, count))
-    direct, exchange = direct_terms(
-        slots, onehot, flags, row_vc, col_vc, coulomb[None, :],
-        val_pairs.transpose(1, 2, 0), cond_pairs.transpose(1, 2, 0), screened,
+    val_t = val_pairs.transpose(1, 2, 0)
+    cond_t = cond_pairs.transpose(1, 2, 0)
+    onehot, _, place, crowd, h10, extra, second, rows = prepare(q_index.reshape(1, count), val_t, cond_t, row_vc)
+    slot, chip = place[0] & 3, place[0] >> 2
+
+    def move(slots, *args):
+        direct, exchange = direct_terms(slots, *args)
+        return direct[((chip >> 2) * slots + slot) * 4 + (chip & 3)], exchange
+
+    direct, exchange = lax.cond(
+        crowd[0, 0] > 0.5, functools.partial(move, 4), functools.partial(move, 3),
+        onehot, rows, col_vc, coulomb[None, :], h10, extra, second, cond_t, screened,
     )
-    direct = direct[place].reshape(count, 4, 4, 4, 4).transpose(0, 3, 1, 4, 2).reshape(count, 256)
+    direct = direct.reshape(count, 4, 4, 4, 4).transpose(0, 3, 1, 4, 2).reshape(count, 256)
     exchange = exchange.reshape(16, 16, 8, 16).transpose(0, 2, 1, 3).reshape(count, 256)
     return 2.0 * exchange - direct
 

time: 270 us -> 221 us (0.82)
  Pallas kernels: 261 us -> 208 us
  local copies, waits for them, and re-layouts: 4.78 us -> 8.88 us
    pallas_call x1, Pallas kernels: 261 us -> 174 us  [direct_terms(): pl.pallas_call(functools.partial(place_kernel, slots), out_shape=(jax.Sha...]
    pallas_call x0 -> x1, Pallas kernels: none -> 34.1 us  [prepare(): pl.pallas_call(prepare_kernel, out_shape=(jax.ShapeDtypeStruct((256, coun...]
    unnamed x3 -> x10, local copies, waits for them, and re-layouts: 0.97 us -> 3.94 us
where the time goes in v3:
time: 221 us
  Pallas kernels  208 us (94%)
  local copies, waits for them, and re-layouts  8.88 us (4%)
  other arithmetic  2.85 us (1%)
    pallas_call x1, Pallas kernels, direct_terms(): pl.pallas_call(functools.partial(place_kernel, slots), out_shape=(jax.Sha...  174 us
    pallas_call x1, Pallas kernels, prepare(): pl.pallas_call(prepare_kernel, out_shape=(jax.ShapeDtypeStruct((256, coun...  34.1 us

profile of v3, /device:TPU:0, one launch (start us, length us, event | category | flops | bytes accessed | tf_op | source)
XLA Modules:
  0.0 221.2 jit_solution(6391202401819983979)
XLA Ops:
  0.0 0.0 copy-start
  0.0 2.4 %copy-done = bf16[128,16,1200]{0,2,1:T(8,128)(2,1)S(1)} copy-done((bf16[128,16,1200]{0,2,1:T(8,128)(2,1)S(1)}, bf16[128,16,1200]{0,2,1:T(8,128)(2,1)}, u32[]{:S(2)}) %copy-start) | copy-done | bytes 4915224
  2.4 0.0 copy-start.1
  2.4 0.9 copy-done.1
  3.3 0.0 copy-start.2
  3.3 0.7 copy-done.2
  3.9 34.1 %shard_map.73 = (bf16[256,128]{1,0:T(8,128)(2,1)}, bf16[16,128]{1,0:T(8,128)(2,1)}, s32[1,128]{1,0:T(1,128)S(1)}, f32[8,128]{1,0:T(8,128)S(1)}, bf16[3,4,4,4,16,...) custom-call(s32[1,128]{1,0:T(1,128)S(1)} %bitcast.28, ...), custom_call_target="tpu_custom_call" | custom-call | tf_op jit(solution)/shard_map/pallas_call | solution.py:191
  38.1 0.6 and_bitcast_fusion
  38.7 0.0 copy-done.4
  38.7 0.5 slice.3
  39.8 0.0 copy-done.3
  39.8 177.6 %conditional.1 = (f32[128,256]{1,0:T(8,128)}, f32[256,128]{1,0:T(8,128)}) conditional(s32[]{:T(128)} %bitcast.3, (bf16[256,128]{1,0:T(8,128)(2,1)}, bf16[8,2,16,1200]{3,2,1,0:T(8,128)(2,1)}, bf16[8,16,1200]{2,1,0:T(8,128)(2,1)}, f32[1,1200]{1,0:T(1,128)S(1)}, bf16[3,4,4,4,16,640]{5,4,3,2,1,0:T(8,128)(2,1)}, ...), branch_computations={%region_0.0_spmd, %region_1.0_spmd} | conditional | flops 2176 | bytes 793104 | solution.py:609
  40.0 174.4 %branch_0_fun.1 = (f32[4,4,3,4,2,128]{5,4,3,2,1,0:T(2,128)}, f32[256,128]{1,0:T(8,128)}, bf16[1,4,4,4,16,640]{5,4,3,2,1,0:T(8,128)(2,1)}, bf16[3,4,4,4,16,640]{5...) custom-call(bf16[256,128]{1,0:T(8,128)(2,1)} %get-tuple-element.49.o, ...), custom_call_target="tpu_custom_call" | custom-call | tf_op jit(solution)/shard_map/cond/branch_0_fun/pallas_call | solution.py:557
  214.4 0.9 copy.23
  215.4 0.7 compare_select_fusion
  216.0 1.4 gather_fusion
  217.4 0.9 broadcast_multiply_fusion
  218.4 0.3 mul.29
  218.7 0.2 copy.25
  218.9 0.4 mul.31
  219.3 1.0 copy.15
  220.3 0.1 copy.16
  220.4 0.1 copy.17
  220.5 0.7 sub.3
  (4 shorter events, 0.0 us)
Async XLA Ops:
  0.0 2.4 %copy-start = (bf16[128,16,1200]{0,2,1:T(8,128)(2,1)S(1)}, bf16[128,16,1200]{0,2,1:T(8,128)(2,1)}, u32[]{:S(2)}) copy-start(bf16[128,16,1200]{0,2,1:T(8,128)(2,1)} %param.11) | copy-start | bytes 14745604
  2.4 0.9 copy-start.1
  3.3 0.7 copy-start.2
  3.9 34.7 %copy-start.4 = (f32[1200]{0:T(1024)S(1)}, f32[1200]{0:T(1024)}, u32[]{:S(2)}) copy-start(f32[1200]{0:T(1024)} %param.14) | copy-start | bytes 14404
  3.9 35.9 %copy-start.3 = (bf16[1,1200,1200]{2,1,0:T(8,128)(2,1)S(1)}, bf16[1,1200,1200]{2,1,0:T(8,128)(2,1)}, u32[]{:S(2)}) copy-start(bf16[1,1200,1200]{2,1,0:T(8,128)(2,1)} %param.15) | copy-start | bytes 8640004

commit v4 on v2

v4 whole, which is shorter than its diff:
```python
import functools

import jax
import jax.numpy as jnp
from jax import lax
from jax.experimental import pallas as pl
from jax.experimental.pallas import tpu as pltpu
from jax.sharding import PartitionSpec as P

MESH = pl.DeviceIdType.MESH
Z, Y, X = 0, 1, 2
ORDERS = ((X, Y, Z), (Y, Z, X), (Z, X, Y))
MAIN = 1152
TILE = 128
WIDTHS = (640, 640, 640, 512)
CUTS = ((0, 256, 512, 640), (0, 128, 384, 640), (0, 256, 384, 640), (0, 128, 256, 512))
NT = (((1,), (1,)), ((), ()))


def streams(slots, r):
    if slots == 3:
        return [(j, ORDERS[j], 0, WIDTHS[r]) for j in range(3)]
    return [(0, ORDERS[i], CUTS[r][i], CUTS[r][i + 1]) for i in range(3)]


def at_axis(ref, lead, axis, index, c0=None, c1=None):
    where = [slice(None)] * 3
    where[axis] = index
    return ref.at[(lead, *where, slice(None), slice(c0, c1))]


def fill_slots(buf, st, onehot, slots, tile, chunk_of):
    per = 64 * 16
    for row in range(16):
        st[pl.ds(row, 64 * slots, stride=16), :] = lax.dot_general(
            onehot[: 64 * slots, :], chunk_of(row), NT, preferred_element_type=jnp.float32
        )
    for j in range(slots):
        buf[j, :, :, :, :, pl.ds(pl.multiple_of(tile * TILE, TILE), TILE)] = (
            st[j * per : (j + 1) * per].astype(jnp.bfloat16).reshape(4, 4, 4, 16, TILE)
        )


def find_places(q_ref, onehot, flag_ref, place_ref, votes):
    size = q_ref.shape[1]
    along = jnp.broadcast_to(q_ref[...], (size, size))
    before = lax.broadcasted_iota(jnp.int32, (size, size), 0) < lax.broadcasted_iota(jnp.int32, (size, size), 1)

    def turned(a):
        return jnp.transpose(a.astype(jnp.float32)).astype(jnp.int32)

    down = turned(along)
    repeat = jnp.sum(jnp.where((along == down) & before, 1.0, 0.0), axis=0, keepdims=True)
    repeats = jnp.broadcast_to(repeat, (size, size)).astype(jnp.int32)
    both = ((along >> 1) == (down >> 1)) & before & (repeats > 0) & (turned(repeats) > 0)
    more = jnp.sum(jnp.where(both, 1.0, 0.0), axis=0, keepdims=True)
    q = q_ref[...]
    core, x, z, y = q & 1, (q >> 1) & 3, (q >> 3) & 3, (q >> 5) & 3
    slot = jnp.where(repeat > 0.5, 2 + more.astype(jnp.int32), core)
    place_ref[...] = slot + ((((y * 4 + x) * 4) + z) << 2)
    flag_ref[...] = jnp.broadcast_to(core.astype(jnp.float32), (16, size)).astype(jnp.bfloat16)
    spots = lax.broadcasted_iota(jnp.int32, onehot.shape, 0)
    onehot[...] = jnp.where(spots == slot * 64 + (z * 4 + y) * 4 + x, 1.0, 0.0).astype(jnp.bfloat16)
    votes[0] = jnp.broadcast_to(jnp.max(more, axis=1, keepdims=True), (8, TILE))


def place_kernel(slots, *refs):
    whole = slots == 3
    if whole:
        (q_ref, rows_hbm, cols_ref, coulomb_ref, val_hbm, cond_hbm, w_hbm,
         out_ref, ex_ref, onehot, flag_ref, place_ref, crowd_ref), refs = refs[:13], refs[13:]
    else:
        (onehot, flag_ref, val_hbm, cond_hbm, w_hbm, out_ref), refs = refs[:6], refs[6:]
    (h10, h11, h12, h13, h20, h21, h22, h23,
     vt, ct, bounce, s0, s1, s2, s3, f0, f1, f2, f3, w2, wt, st, tt, zbuf, ybuf, dbuf,
     in_sem, w_sem, send, recv, last, local, local_on, back_send, back_recv), refs = refs[:35], refs[35:]
    if whole:
        rows, votes, sums, row_sem, one_sem, two_sem = refs
    kb = lax.axis_index("kb")
    col = lax.axis_index("col")
    here = (kb & 3, kb >> 2, col >> 1)
    core = col & 1

    def dev(chip, which):
        return (chip[Y] * 4 + chip[Z], chip[X] * 2 + which)

    def moved(axis, index):
        chip = list(here)
        chip[axis] = index
        return tuple(chip)

    load_val = pltpu.make_async_copy(val_hbm, vt, in_sem.at[0])
    load_val.start()
    load_tail = pltpu.make_async_copy(cond_hbm.at[:, MAIN:], ct, in_sem.at[1])
    load_tail.start()
    load_w = pltpu.make_async_copy(w_hbm.at[0], w2.at[core], in_sem.at[2])
    load_w.start()

    barrier = pltpu.get_barrier_semaphore()
    for axis in range(3):
        for d in (1, 2, 3):
            for which in range(2):
                pl.semaphore_signal(
                    barrier, inc=1, device_id=dev(moved(axis, (here[axis] + d) & 3), which), device_id_type=MESH
                )
    pl.semaphore_signal(barrier, inc=1, device_id=dev(here, 1 - core), device_id_type=MESH)

    def across(dy, dx):
        return (here[Z], (here[Y] + dy) & 3, (here[X] + dx) & 3)

    for dy in (1, 2, 3):
        for dx in (1, 2, 3):
            pl.semaphore_signal(barrier, inc=1, device_id=dev(across(dy, dx), core), device_id_type=MESH)

    def mate(d):
        return (kb, (col + d) & 7)

    def far(d):
        return (((kb >> 2) + (d >> 2) & 3) * 4 + ((kb + d) & 3), col)

    if whole:
        for d in range(5, 16):
            if d & 3:
                pl.semaphore_signal(barrier, inc=1, device_id=far(d), device_id_type=MESH)
        load_rows = pltpu.make_async_copy(rows_hbm, rows.at[col], in_sem.at[3])
        load_rows.start()
        find_places(q_ref, onehot, flag_ref, place_ref, votes)

    rounds = ((s0, h10, h20, f0), (s1, h11, h21, f1), (s2, h12, h22, f2), (s3, h13, h23, f3))
    parts = tuple(streams(slots, r) for r in range(4))
    n_streams = 3

    def build(buf, first, tiles):
        @pl.loop(0, tiles)
        def _(t):
            fill_slots(buf, st, onehot, slots, t, lambda row: vt[row, pl.ds(pl.multiple_of((first + t) * TILE, TILE), TILE), :])

    def held(r, j, k):
        return rounds[r][k], j

    def ring(r, s, k, d):
        j, order, c0, c1 = parts[r][s]
        axis = order[k]
        there = (here[axis] + d) & 3
        return pltpu.make_async_remote_copy(
            at_axis(*held(r, j, k), axis, there, c0, c1),
            at_axis(*held(r, j, k + 1), axis, here[axis], c0, c1),
            send.at[r, s, k, d], recv.at[r, s, k, d],
            device_id=dev(moved(axis, there), core), device_id_type=MESH,
        )

    def keep(r, s, k):
        j, order, c0, c1 = parts[r][s]
        axis = order[k]
        src = at_axis(*held(r, j, k), axis, here[axis], c0, c1)
        dst = at_axis(*held(r, j, k + 1), axis, here[axis], c0, c1)
        if k == 0:
            return (pltpu.make_async_copy(src, dst, local.at[r, s, k]),)
        via = bounce.at[r % 2, j, :, :, :, c0:c1]
        return (
            pltpu.make_async_copy(src, via, local.at[r, s, k]),
            pltpu.make_async_copy(via, dst, local_on.at[r, s, k]),
        )

    def start_ring(r, k, lo=0, hi=n_streams):
        for d in (1, 3, 2):
            for s in range(lo, hi):
                ring(r, s, k, d).start()
        for s in range(lo, hi):
            keep(r, s, k)[0].start()

    def wait_ring(r, k, lo=0, hi=n_streams):
        for s in range(lo, hi):
            own = keep(r, s, k)
            own[0].wait()
            if len(own) > 1:
                own[1].start()
        for s in range(lo, hi):
            for d in (1, 3, 2):
                c = ring(r, s, k, d)
                c.wait_send()
                c.wait_recv()
            own = keep(r, s, k)
            if len(own) > 1:
                own[1].wait()

    def final(r, s, d):
        j, order, c0, c1 = parts[r][s]
        axis = order[2]
        there = (here[axis] + d) & 3
        lead, goal = (core, j) if whole and j < 2 else (j, core)
        sem = last.at[r, lead, d] if whole and j < 2 else last.at[r, s, d]
        return pltpu.make_async_remote_copy(
            at_axis(rounds[r][2], j, axis, there, c0, c1),
            at_axis(rounds[r][3], lead, axis, here[axis], c0, c1),
            send.at[r, s, 2, d], sem,
            device_id=dev(moved(axis, there), goal), device_id_type=MESH,
        )

    def final_local(r, s):
        j, order, c0, c1 = parts[r][s]
        axis = order[2]
        lead = core if whole and j < 2 else j
        return pltpu.make_async_copy(
            at_axis(rounds[r][2], j, axis, here[axis], c0, c1),
            at_axis(rounds[r][3], lead, axis, here[axis], c0, c1),
            local.at[r, s, 2],
        )

    def start_final(r):
        for d in (1, 3, 2):
            for s in range(n_streams):
                final(r, s, d).start()
        for s in range(n_streams):
            if whole and s < 2:
                @pl.when(core == s)
                def _():
                    final_local(r, s).start()

                @pl.when(core != s)
                def _():
                    final(r, s, 0).start()
            else:
                final_local(r, s).start()

    def wait_final(r):
        for s in range(n_streams):
            for d in (1, 3, 2):
                final(r, s, d).wait_send()
            if whole and s < 2:
                @pl.when(core == s)
                def _():
                    final_local(r, s).wait()

                @pl.when(core != s)
                def _():
                    final(r, s, 0).wait_send()
            else:
                final_local(r, s).wait()
                for d in (1, 3, 2):
                    final(r, s, d).wait_recv()
        for mine in range(2 if whole else 0):
            axis = ORDERS[mine][2]

            @pl.when(core == mine)
            def _():
                for lead in range(2):
                    for d in (1, 3, 2) if lead == mine else (1, 3, 2, 0):
                        at = at_axis(rounds[r][3], lead, axis, here[axis])
                        pltpu.make_async_remote_copy(
                            at, at, send.at[r, mine, 2, d], last.at[r, lead, d],
                            device_id=dev(here, 1 - core), device_id_type=MESH,
                        ).wait_recv()

    def vote(d):
        return pltpu.make_async_remote_copy(
            votes.at[0], votes.at[d], one_sem.at[0, d], one_sem.at[1, d], device_id=mate(d), device_id_type=MESH
        )

    def count_votes(d):
        return pltpu.make_async_remote_copy(
            sums.at[0], sums.at[d], two_sem.at[0, d], two_sem.at[1, d], device_id=far(d), device_id_type=MESH
        )

    def row_copy(d):
        return pltpu.make_async_remote_copy(
            rows_hbm, rows.at[col], row_sem.at[0, d], row_sem.at[1, d], device_id=mate(d), device_id_type=MESH
        )

    pl.semaphore_wait(barrier, 37 if whole else 28)
    if whole:
        for d in range(1, 8):
            vote(d).start()
        for d in range(1, 8):
            row_copy(d).start()
    load_val.wait()
    build(s0, 0, 5)
    start_ring(0, 0)
    load_tail.wait()
    build(s1, 5, 4)
    gap = jnp.zeros((16, TILE), jnp.bfloat16)
    fill_slots(
        s1, st, onehot, slots, 4,
        lambda row: jnp.concatenate([vt[row, MAIN:, :], gap, ct[row], flag_ref[...]], axis=0),
    )
    load_cond = pltpu.make_async_copy(cond_hbm, vt, in_sem.at[0])
    load_cond.start()
    start_ring(1, 0)
    send_w = pltpu.make_async_remote_copy(
        w_hbm.at[0], w2.at[core], w_sem.at[0], w_sem.at[1], device_id=dev(here, 1 - core), device_id_type=MESH
    )
    send_w.start()
    if whole:
        for d in range(1, 8):
            vote(d).wait()
        sums[0] = jnp.max(votes[...], axis=0)
        for d in range(1, 16):
            count_votes(d).start()
    load_cond.wait()
    build(s2, 0, 5)
    wait_ring(0, 0)
    start_ring(0, 1)
    start_ring(2, 0)
    build(s3, 5, 4)
    wait_ring(1, 0)
    start_ring(1, 1)
    start_ring(3, 0)

    if whole:
        load_rows.wait()
        for d in range(1, 8):
            row_copy(d).wait()
        scaled = (cols_ref[...].astype(jnp.float32) * coulomb_ref[...][None]).astype(jnp.bfloat16)
        ex_ref[...] = lax.dot_general(
            rows[...].reshape(256, 1200), scaled.reshape(128, 1200), NT, preferred_element_type=jnp.float32
        )
        for d in range(1, 16):
            count_votes(d).wait()
        crowd_ref[...] = jnp.max(sums[...], axis=0)
    load_w.wait()
    send_w.wait()
    wt[...] = jnp.zeros_like(wt)
    for which in range(2):
        wt[which, 64:112] = w2[which, MAIN:]

    wait_ring(0, 1)
    start_final(0)
    wait_ring(2, 0)
    start_ring(2, 1)
    wait_ring(1, 1)
    start_final(1)
    wait_ring(3, 0)
    start_ring(3, 1)
    wait_ring(2, 1)
    start_final(2)
    wait_final(0)
    wait_ring(3, 1)
    start_final(3)
    wait_final(1)

    group = lax.broadcasted_iota(jnp.int32, (16, 256), 1) >> 4
    line = lax.broadcasted_iota(jnp.int32, (16, 256), 0)

    def diagonal(full):
        total = jnp.zeros((16, 256), jnp.float32)
        for i in range(16):
            total = jnp.where(group == i, full[16 * i : 16 * i + 16], total)
        return total

    def apply(i, times):
        b, z = i >> 2, i & 3
        tail = f1[b, z].reshape(256, 640)
        x = jnp.concatenate([f0[b, z].reshape(256, 640), tail], axis=1)[:, :1200]
        for n, (g0, size) in enumerate(((0, 256), (256, 256), (512, 128), (640, 256), (896, 256), (0, 0))):
            part = times(b, x, tail, g0, size).astype(jnp.bfloat16)
            if size == 0:
                s1[b, z, :, :, :, 512:640] = part.reshape(4, 4, 16, 128)
                tt[b, z] = diagonal(lax.dot_general(tail[:, 512:], part, NT, preferred_element_type=jnp.float32))
            else:
                to, at = (s0, g0) if g0 < 640 else (s1, g0 - 640)
                to[b, z, :, :, :, at : at + size] = part.reshape(4, 4, 16, size)

    def one(which, x, g0, size):
        w = w2[which, g0 : g0 + size, :] if size else wt[which]
        return lax.dot_general(x, w, NT, preferred_element_type=jnp.float32)

    fixed = 8 if whole else 0

    @pl.loop(0, fixed)
    def _(i):
        apply(i, lambda b, x, tail, g0, size: one(core, x, g0, size))

    def either(b, x, tail, g0, size):
        flag = tail[:, 624:625].astype(jnp.float32) > 0.5
        return jnp.where(flag, one(1, x, g0, size), one(0, x, g0, size))

    @pl.loop(fixed, 4 * slots)
    def _(i):
        apply(i, either)

    wait_final(2)

    @pl.loop(0, 4 * slots)
    def _(i):
        b, z = i >> 2, i & 3
        full = lax.dot_general(
            f2[b, z].reshape(256, 640), s0[b, z].reshape(256, 640), NT, preferred_element_type=jnp.float32
        )
        tt[b, z] = tt[b, z] + diagonal(full)

    wait_final(3)

    @pl.loop(0, 4 * slots)
    def _(i):
        b, z = i >> 2, i & 3
        full = lax.dot_general(
            f3[b, z].reshape(256, 512),
            s1[b, z, :, :, :, :512].reshape(256, 512),
            NT,
            preferred_element_type=jnp.float32,
        )
        got = diagonal(full) + tt[b, z]
        turned = jnp.where(group == line, got, 0.0)
        for k in range(1, 16):
            shifted = pltpu.roll(pltpu.roll(got, 16 - k, 0), 16 * k, 1)
            turned = jnp.where(group == ((line + k) & 15), shifted, turned)
        for slot in range(16):
            zbuf[b, z, slot >> 2, slot & 3, 0:1] = turned[slot : slot + 1, :128]
            zbuf[b, z, slot >> 2, slot & 3, 1:2] = turned[slot : slot + 1, 128:]
        back_core = jnp.where(b < 2, b, core) if whole else core
        mine = (z == here[Z]) & (back_core == core)
        src = zbuf.at[b, z]
        dst = ybuf.at[:, :, jnp.where(b < 2, core, b) if whole else 0, here[Z]]

        @pl.when(mine)
        def _():
            pltpu.make_async_copy(src, dst, back_recv.at[0]).start()

        @pl.when(jnp.logical_not(mine))
        def _():
            pltpu.make_async_remote_copy(
                src, dst, back_send.at[0], back_recv.at[0],
                device_id=dev(moved(Z, z), back_core), device_id_type=MESH,
            ).start()

    pltpu.make_async_copy(ybuf, ybuf, back_recv.at[0]).wait()
    back_own = pltpu.make_async_copy(ybuf.at[here[Y], here[X]], dbuf.at[here[Y], here[X]], back_recv.at[16])
    back_own.start()

    def back(dy, dx):
        chip = across(dy, dx)
        return pltpu.make_async_remote_copy(
            ybuf.at[chip[Y], chip[X]], dbuf.at[here[Y], here[X]],
            back_send.at[4 * dy + dx], back_recv.at[4 * dy + dx],
            device_id=dev(chip, core), device_id_type=MESH,
        )

    ways = [(dy, dx) for dy in (2, 1, 3, 0) for dx in (2, 1, 3, 0) if dy or dx]
    for way in ways:
        back(*way).start()
    back_own.wait()
    for way in ways:
        back(*way).wait()

    @pl.loop(0, 4 * slots - (2 if whole else 1))
    def _(_):
        pltpu.make_async_copy(zbuf.at[0, 0], zbuf.at[0, 0], back_send.at[0]).wait()

    out_ref[...] = dbuf[...]


def direct_terms(slots, *args):
    hbm = pl.BlockSpec(memory_space=pl.ANY)
    vmem = pl.BlockSpec(memory_space=pltpu.VMEM)
    bf16, f32 = jnp.bfloat16, jnp.float32
    whole = slots == 3
    count = args[-2].shape[2]
    wide = [(slots, 4, 4, 4, 16, w) for w in WIDTHS]
    back = (4, 4, slots, 4, 2, 128)
    dma = pltpu.SemaphoreType.DMA
    shape = jax.ShapeDtypeStruct
    small = [shape(back, f32)]
    extra = []
    if whole:
        small += [
            shape((256, 128), f32), shape((256, count), bf16), shape((16, count), bf16),
            shape((1, count), jnp.int32), shape((8, TILE), f32),
        ]
        extra = [
            pltpu.VMEM((8,) + args[1].shape, bf16), pltpu.VMEM((8, 8, TILE), f32), pltpu.VMEM((16, 8, TILE), f32),
            dma((2, 8)), dma((2, 8)), dma((2, 16)),
        ]
    out = pl.pallas_call(
        functools.partial(place_kernel, slots),
        out_shape=(*small, *(shape(w, bf16) for w in wide), *(shape(w, bf16) for w in wide)),
        in_specs=[vmem, hbm, vmem, vmem, hbm, hbm, hbm] if whole else [vmem, vmem, hbm, hbm, hbm],
        out_specs=(vmem,) * len(small) + (hbm,) * 8,
        scratch_shapes=[
            pltpu.VMEM((16, 1200, count), bf16),
            pltpu.VMEM((16, 1200 - MAIN, count), bf16),
            pltpu.VMEM((2, slots, 4, 4, 16, WIDTHS[0]), bf16),
            *(pltpu.VMEM(w, bf16) for w in wide),
            *(pltpu.VMEM(w, bf16) for w in wide),
            pltpu.VMEM((2, 1200, 1200), bf16),
            pltpu.VMEM((2, TILE, 1200), bf16),
            pltpu.VMEM((slots * 64 * 16, TILE), f32),
            pltpu.VMEM((slots, 4, 16, 256), f32),
            pltpu.VMEM((slots, 4, 4, 4, 2, 128), f32),
            pltpu.VMEM(back, f32),
            pltpu.VMEM(back, f32),
            dma((4,)),
            dma((2,)),
            dma((4, 3, 3, 4)),
            dma((4, 3, 2, 4)),
            dma((4, 3, 4)),
            dma((4, 3, 3)),
            dma((4, 3, 3)),
            dma((17,)),
            dma((17,)),
            *extra,
        ],
        compiler_params=pltpu.CompilerParams(
            collective_id=slots, has_side_effects=True, vmem_limit_bytes=56 * 2**20
        ),
    )(*args)
    return (out[0].reshape(slots * 64, 256), *out[1 : len(small)])


def shards(q_index, cond_pairs, val_pairs, row_vc, col_vc, coulomb, screened):
    count = cond_pairs.shape[0]
    val_t = val_pairs.transpose(1, 2, 0)
    cond_t = cond_pairs.transpose(1, 2, 0)
    direct, exchange, onehot, flags, place, crowd = direct_terms(
        3, q_index.reshape(1, count), row_vc, col_vc, coulomb[None, :], val_t, cond_t, screened
    )

    def left(*args):
        return direct_terms(1, *args)[0]

    def none(*args):
        return jnp.zeros((64, 256), jnp.float32)

    rest = lax.cond(crowd[0, 0] > 0.5, left, none, onehot[192:], flags, val_t, cond_t, screened)
    slot, chip = place[0] & 3, place[0] >> 2
    at = jnp.where(slot < 3, ((chip >> 2) * 3 + slot) * 4 + (chip & 3), 192 + chip)
    direct = jnp.concatenate([direct, rest], axis=0)[at]
    direct = direct.reshape(count, 4, 4, 4, 4).transpose(0, 3, 1, 4, 2).reshape(count, 256)
    exchange = exchange.reshape(16, 16, 8, 16).transpose(0, 2, 1, 3).reshape(count, 256)
    return 2.0 * exchange - direct


def solution(mesh):
    return jax.shard_map(
        shards,
        mesh=mesh,
        in_specs=(
            P(("kb", "col"), None),
            P(("kb", "col"), None, None),
            P(("kb", "col"), None, None),
            P(("kb", "col"), None, None),
            P("col", None, None),
            P(),
            P(("kb", "col"), None, None),
        ),
        out_specs=P(("kb", "col"), None),
        check_vma=False,
    )
```

time: 270 us -> 291 us (1.078)
  Pallas kernels: 261 us -> 282 us
    pallas_call x1 -> x2, Pallas kernels: 261 us -> 282 us  [direct_terms(): pl.pallas_call(functools.partial(place_kernel, slots), out_shape=(*small,...]
where the time goes in v4:
time: 291 us
  Pallas kernels  282 us (97%)
  local copies, waits for them, and re-layouts  6.82 us (2%)
    pallas_call x2, Pallas kernels, direct_terms(): pl.pallas_call(functools.partial(place_kernel, slots), out_shape=(*small,...  282 us

profile of v4, /device:TPU:0, one launch (start us, length us, event | category | flops | bytes accessed | tf_op | source)
XLA Modules:
  0.0 291.0 jit_solution(8516396750231694143)
XLA Ops:
  0.0 1.3 broadcast_in_dim.4.refs_3_
  1.3 0.0 copy-start
  1.3 196.7 %shard_map.73 = (f32[4,4,3,4,2,128]{5,4,3,2,1,0:T(2,128)}, f32[256,128]{1,0:T(8,128)}, bf16[256,128]{1,0:T(8,128)(2,1)S(1)}, bf16[16,128]{1,0:T(8,128)(2,1)S(1)}...) custom-call(s32[1,128]{1,0:T(1,128)} %bitcast.42, ...), custom_call_target="tpu_custom_call" | custom-call | tf_op jit(solution)/shard_map/pallas_call | solution.py:473
  198.0 1.2 slice.7
  199.9 0.9 broadcast_multiply_fusion
  200.8 0.9 copy.25
  201.7 0.0 copy-done
  201.7 0.0 copy-start.1
  201.8 86.5 %conditional.1 = (f32[64,256]{1,0:T(8,128)S(1)}) conditional(s32[]{:T(128)} %bitcast.4, () %tuple.11, (bf16[256,128]{1,0:T(8,128)(2,1)S(1)}, bf16[16,128]{1,0:T(8,128)(2,1)S(1)}, bf16[16,1200,128]{2,1,0:T(8,128)(2,1)}, bf16[16,1200,128]{2,1,0:T(8,128)(2,1)}, bf16[1,1200,1200]{2,1,0:T(8,128)(2,1)S(1)}) %tuple.17), branch_computations={%region_0.0_spmd, %region_1.0_spmd} | conditional | bytes 163848 | solution.py:523
  202.0 0.6 slice.5.refs_0_
  202.6 84.8 %branch_1_fun.1 = (f32[4,4,1,4,2,128]{5,4,3,2,1,0:T(2,128)}, bf16[1,4,4,4,16,640]{5,4,3,2,1,0:T(8,128)(2,1)}, bf16[1,4,4,4,16,640]{5,4,3,2,1,0:T(8,128)(2,1)}, b...) custom-call(bf16[64,128]{1,0:T(8,128)(2,1)} %slice.5.refs_0_, ...), custom_call_target="tpu_custom_call" | custom-call | tf_op jit(solution)/shard_map/cond/branch_1_fun/pallas_call | solution.py:473
  287.4 0.8 copy.23
  288.3 0.0 copy-done.1
  288.3 0.8 gather_fusion
  289.1 0.1 copy.15
  289.2 0.1 copy.16
  289.2 0.1 copy.17
  289.3 0.3 mul.41
  289.7 0.2 copy.24
  289.9 0.4 mul.43
  290.3 0.7 sub.3
  (3 shorter events, 0.0 us)
Async XLA Ops:
  1.3 200.4 %copy-start = (bf16[1,1200,1200]{2,1,0:T(8,128)(2,1)S(1)}, bf16[1,1200,1200]{2,1,0:T(8,128)(2,1)}, u32[]{:S(2)}) copy-start(bf16[1,1200,1200]{2,1,0:T(8,128)(2,1)} %refs_6_.1) | copy-start | bytes 8640004
  201.7 86.5 %copy-start.1 = (s32[1,128]{1,0:T(1,128)S(1)}, s32[1,128]{1,0:T(1,128)}, u32[]{:S(2)}) copy-start(s32[1,128]{1,0:T(1,128)} %get-tuple-element.36) | copy-start | bytes 1540

commit v5 on v2

--- a/solution.py
+++ b/solution.py
@@ -192,9 +192,18 @@
                             device_id=dev(here, 1 - core), device_id_type=MESH,
                         ).wait_recv()
 
+    pl.semaphore_wait(barrier, 19)
+    def row_copy(d):
+        to = lax.rem(col + d, 8)
+        return pltpu.make_async_remote_copy(
+            rows_hbm, rows.at[col], row_sem.at[0, d], row_sem.at[1, d], device_id=(kb, to), device_id_type=MESH
+        )
+
+    for d in range(1, 8):
+        row_copy(d).start()
+
     load_val.wait()
     build(s0, 0, 5)
-    pl.semaphore_wait(barrier, 19)
     start_ring(0, 0)
     load_tail.wait()
     build(s1, 5, 4)
@@ -208,15 +217,6 @@
         w_hbm.at[0], w2.at[core], w_sem.at[0], w_sem.at[1], device_id=dev(here, 1 - core), device_id_type=MESH
     )
     send_w.start()
-
-    def row_copy(d):
-        to = lax.rem(col + d, 8)
-        return pltpu.make_async_remote_copy(
-            rows_hbm, rows.at[col], row_sem.at[0, d], row_sem.at[1, d], device_id=(kb, to), device_id_type=MESH
-        )
-
-    for d in range(1, 8):
-        row_copy(d).start()
 
     load_cond.wait()
     build(s2, 0, 5)

time: 270 us -> 265 us (0.981)
  Pallas kernels: 261 us -> 256 us
    pallas_call x1, Pallas kernels: 261 us -> 256 us  [direct_terms(): pl.pallas_call(functools.partial(place_kernel, slots), out_shape=(jax.Sha...]
where the time goes in v5:
time: 265 us; the launch traced here: 264 us
  Pallas kernels  256 us (97%)
  local copies, waits for them, and re-layouts  4.78 us (2%)
  other arithmetic  3.83 us (1%)
    pallas_call x1, Pallas kernels, direct_terms(): pl.pallas_call(functools.partial(place_kernel, slots), out_shape=(jax.Sha...  256 us

profile of v5, /device:TPU:0, one launch (start us, length us, event | category | flops | bytes accessed | tf_op | source)
XLA Modules:
  0.0 264.5 jit_solution(3623312717445749225)
XLA Ops:
  0.0 0.9 convert_reduce_fusion
  0.9 0.7 and_convert_fusion
  1.6 0.7 fusion.onehot
  2.2 0.6 broadcast_in_dim.4.flag_ref
  2.8 1.3 broadcast_in_dim.5.coulomb_ref
  4.1 0.0 copy-start
  4.1 255.8 %shard_map.73 = (f32[4,4,4,4,2,128]{5,4,3,2,1,0:T(2,128)}, f32[256,128]{1,0:T(8,128)}, bf16[4,4,4,4,16,640]{5,4,3,2,1,0:T(8,128)(2,1)}, bf16[4,4,4,4,16,640]{5,4...) custom-call(bf16[256,128]{1,0:T(8,128)(2,1)} %fusion.onehot, ...), custom_call_target="tpu_custom_call" | custom-call | tf_op jit(solution)/shard_map/pallas_call | solution.py:390
  259.9 1.0 copy.26
  260.9 0.0 copy-done
  260.9 0.8 gather_fusion
  261.7 0.1 copy.19
  261.7 0.1 copy.20
  261.8 0.1 copy.21
  261.9 0.9 broadcast_multiply_fusion
  262.8 0.3 mul.78
  263.1 0.2 copy.25
  263.3 0.4 mul.80
  263.8 0.7 sub.3
  (2 shorter events, 0.0 us)
Async XLA Ops:
  4.1 256.7 %copy-start = (s32[128,1]{0,1:T(1,128)S(1)}, s32[128,1]{0,1:T(1,128)}, u32[]{:S(2)}) copy-start(s32[128,1]{0,1:T(1,128)} %param.7) | copy-start | bytes 1540
